TPU v7x, 32 devices: a whole 2x2x4 slice. The times are simulated.
32 devices in a mesh: dp: 8 (over z, x), rows: 4 (over y, core).
Axes of the slice: x: 2, y: 2, z: 4, core: 2. Of those that a mesh axis runs over, the one named last changes fastest.
Arguments:
- input_a: bfloat16 [16, 32, 14, 1024], P('rows', 'dp'), may hold values from -48 to 48
- input_b: bfloat16 [16, 96, 10, 1024], P('rows', 'dp'), may hold values from -48 to 48
- live_views: int32 [8, 2], replicated, may hold values from 2 to 12, as said below
- reduce_one: bfloat16 [1024, 256], replicated, may hold values from -0.1875 to 0.1875
- spatial_one: bfloat16 [256, 3, 3, 256], replicated, may hold values from -0.125 to 0.125
- expand_one: bfloat16 [256, 1024], replicated, may hold values from -0.375 to 0.375
- reduce_two: bfloat16 [1024, 512], replicated, may hold values from -0.1875 to 0.1875
- spatial_two: bfloat16 [512, 3, 3, 512], replicated, may hold values from -0.09375 to 0.09375
- expand_two: bfloat16 [512, 2048], replicated, may hold values from -0.25 to 0.25
- shortcut_two: bfloat16 [1024, 2048], replicated, may hold values from -0.1875 to 0.1875
- gain_narrow: float32 [256], replicated, may hold values from 0.5 to 1.5
- bias_narrow: float32 [256], replicated, may hold values from -0.5 to 0.5
- gain_spatial: float32 [256], replicated, may hold values from 0.5 to 1.5
- bias_spatial: float32 [256], replicated, may hold values from -0.5 to 0.5
- gain_widened: float32 [1024], replicated, may hold values from 0.5 to 1.5
- bias_widened: float32 [1024], replicated, may hold values from -0.5 to 0.5
- gain_squeeze: float32 [512], replicated, may hold values from 0.5 to 1.5
- bias_squeeze: float32 [512], replicated, may hold values from -0.5 to 0.5
- gain_strided: float32 [512], replicated, may hold values from 0.5 to 1.5
- bias_strided: float32 [512], replicated, may hold values from -0.5 to 0.5
- gain_output: float32 [2048], replicated, may hold values from 0.5 to 1.5
- bias_output: float32 [2048], replicated, may hold values from -0.5 to 0.5
- gain_shortcut: float32 [2048], replicated, may hold values from 0.5 to 1.5
- bias_shortcut: float32 [2048], replicated, may hold values from -0.5 to 0.5
- cotangent_a: bfloat16 [8, 32, 7, 2048], P('rows', 'dp'), may hold values from -6 to 6
- cotangent_b: bfloat16 [8, 96, 5, 2048], P('rows', 'dp'), may hold values from -6 to 6
Outputs:
- block_out_a: bfloat16 [8, 32, 7, 2048], P('rows', 'dp')
- block_out_b: bfloat16 [8, 96, 5, 2048], P('rows', 'dp')
- grad_input_a: bfloat16 [16, 32, 14, 1024], P('rows', 'dp')
- grad_input_b: bfloat16 [16, 96, 10, 1024], P('rows', 'dp')
- grad_reduce_one: float32 [1024, 256], P(('dp', 'rows'))
- grad_spatial_one: float32 [256, 3, 3, 256], P(('dp', 'rows'))
- grad_expand_one: float32 [256, 1024], P(('dp', 'rows'))
- grad_reduce_two: float32 [1024, 512], P(('dp', 'rows'))
- grad_spatial_two: float32 [512, 3, 3, 512], P(('dp', 'rows'))
- grad_expand_two: float32 [512, 2048], P(('dp', 'rows'))
- grad_shortcut_two: float32 [1024, 2048], P(('dp', 'rows'))
- grad_gain_narrow: float32 [256], replicated
- grad_bias_narrow: float32 [256], replicated
- grad_gain_spatial: float32 [256], replicated
- grad_bias_spatial: float32 [256], replicated
- grad_gain_widened: float32 [1024], replicated
- grad_bias_widened: float32 [1024], replicated
- grad_gain_squeeze: float32 [512], replicated
- grad_bias_squeeze: float32 [512], replicated
- grad_gain_strided: float32 [512], replicated
- grad_bias_strided: float32 [512], replicated
- grad_gain_output: float32 [2048], replicated
- grad_bias_output: float32 [2048], replicated
- grad_gain_shortcut: float32 [2048], replicated
- grad_bias_shortcut: float32 [2048], replicated
Inputs may be any that keep to these rules, and one draw needn't show every extreme that they name: `live_views`: row d gives the live views in the slots of index d of dp: column 0 for the first group (at most 4), column 1 for the second (at most 12); live views fill the first slots, at least half of them, and in every draw some index holds 4 live views of the first group and some index 12 of the second.
All inputs are finite; a program needn't handle non-finite values.
Results may differ from a plain program's by a relative error of at most 0.023.
Values may be sent and summed in bfloat16 or wider, within the bound.
A program may use at most 192 MiB of HBM per device.

v0:
```python
import jax
import jax.numpy as jnp
from jax import lax
from jax.sharding import PartitionSpec as P

HA = 14
WA = 14
HB = 10
WB = 10


EPS = 1e-05
TAPS = ((0, 0), (0, 1), (1, 0))


def shortened(value):
    return jax.tree.map(lambda a: a.astype(jnp.bfloat16) if a.dtype == jnp.float32 else a, value)


def padded_2(cells, sides, width):
    for axis, dim in sides:
        count = lax.axis_size(axis)
        ends = count - 1
        head = lax.slice_in_dim(cells, 0, width, axis=dim)
        tail = lax.slice_in_dim(cells, cells.shape[dim] - width, cells.shape[dim], axis=dim)
        cells = jnp.concatenate(
            [
                lax.ppermute(tail, axis, [(i, (i + 1) % count) for i in range(ends)]),
                cells,
                lax.ppermute(head, axis, [((i + 1) % count, i) for i in range(ends)]),
            ],
            axis=dim,
        )
    return cells


def passed_along(block, axis, distance):
    devices = range(lax.axis_size(axis))
    route = [(i - distance, i) for i in devices if i - distance in devices]
    return lax.ppermute(block, axis, route)


def silu(value):
    return value * jax.nn.sigmoid(value)


def silu_slope(value):
    sigma = jax.nn.sigmoid(value)
    return sigma * (1.0 + value * (1.0 - sigma))


def apply_matrix(acts, matrix):
    flat = acts.reshape(-1, acts.shape[-1])
    out = jnp.dot(flat, matrix, preferred_element_type=jnp.float32)
    return out.reshape(acts.shape[:-1] + (matrix.shape[1],))


def apply_transpose(grads, matrix):
    flat = grads.reshape(-1, grads.shape[-1])
    out = lax.dot_general(
        flat, matrix, (((1,), (1,)), ((), ())), preferred_element_type=jnp.float32
    )
    return out.reshape(grads.shape[:-1] + (matrix.shape[0],))


def outer_sum(acts, grads):
    return lax.dot_general(
        acts.reshape(-1, acts.shape[-1]),
        grads.reshape(-1, grads.shape[-1]),
        (((0,), (0,)), ((), ())),
        preferred_element_type=jnp.float32,
    )


def strip_mask(live_views, group, rows, views, height):
    column = live_views[:, group]
    live = jnp.sum(jnp.where(jnp.arange(column.shape[0]) == lax.axis_index("dp"), column, 0))
    view_ok = jnp.arange(views) < live
    row_ok = lax.axis_index("rows") * rows + jnp.arange(rows) < height
    return (row_ok[:, None] & view_ok[None, :]).astype(jnp.float32)[:, :, None, None]


def masked_sums(parts, masks):
    total = 0.0
    square = 0.0
    for value, mask in zip(parts, masks):
        kept = value * mask
        total = total + jnp.sum(kept, axis=(0, 1, 2))
        square = square + jnp.sum(kept * value, axis=(0, 1, 2))
    return (total, square)


def shared_sums(parts, masks):
    total, square = masked_sums(parts, masks)
    return lax.psum((total, square), ("dp", "rows"))


def standardize(parts, total, square, count):
    mean = total / count
    scale = lax.rsqrt(square / count - mean * mean + EPS)
    return ([(value - mean) * scale for value in parts], scale)


def slope_sums(slopes, normed):
    first = 0.0
    second = 0.0
    for slope, unit in zip(slopes, normed):
        first = first + jnp.sum(slope, axis=(0, 1, 2))
        second = second + jnp.sum(slope * unit, axis=(0, 1, 2))
    return (first, second)


def shared_grads(slopes, normed):
    first, second = slope_sums(slopes, normed)
    return lax.psum((first, second), ("dp", "rows"))


def norm_back(slopes, normed, masks, scale, gain, first, second, count):
    factor = scale * gain
    return [
        (factor * (slope - first / count - unit * (second / count)) * mask).astype(jnp.bfloat16)
        for slope, unit, mask in zip(slopes, normed, masks)
    ]


def rim_pack(parts):
    return jnp.concatenate(
        [jnp.stack([value[0].reshape(-1), value[-1].reshape(-1)]) for value in parts], axis=1
    )


def rim_split(flat, parts):
    pieces = []
    start = 0
    for value in parts:
        size = value[0].size
        pieces.append(flat[start : start + size].reshape(value.shape[1:]))
        start = start + size
    return pieces


def spatial_same(padded, weight):
    rows = padded.shape[0] - 2
    width = padded.shape[2]
    wide = jnp.pad(padded, ((0, 0), (0, 0), (1, 1), (0, 0)))
    total = 0.0
    for across in range(3):
        for along in range(3):
            total = total + apply_matrix(
                wide[across : across + rows, :, along : along + width], weight[:, across, along]
            )
    return (total, wide)


def spatial_same_back(wide, grads, weight):
    rows = grads.shape[0]
    width = grads.shape[2]
    weight_grad = jnp.stack(
        [
            jnp.stack(
                [
                    outer_sum(wide[across : across + rows, :, along : along + width], grads)
                    for along in range(3)
                ],
                axis=1,
            )
            for across in range(3)
        ],
        axis=1,
    )
    back = 0.0
    for across in range(3):
        for along in range(3):
            term = apply_transpose(grads, weight[:, across, along])
            back = back + jnp.pad(term, ((across, 2 - across), (0, 0), (along, 2 - along), (0, 0)))
    return (weight_grad, back[:, :, 1 : width + 1])


def strided_grid(acts, above):
    rows, views, width, chans = acts.shape
    full = jnp.concatenate([above[None], acts, jnp.zeros_like(above)[None]], axis=0)
    full = jnp.pad(full, ((0, 0), (0, 0), (1, 1), (0, 0)))
    return full.reshape(rows // 2 + 1, 2, views, width // 2 + 1, 2, chans)


def strided_forward(grid, weight):
    out_rows = grid.shape[0] - 1
    out_cols = grid.shape[3] - 1
    total = 0.0
    for across in range(3):
        lead, row_bit = TAPS[across]
        for along in range(3):
            side, col_bit = TAPS[along]
            total = total + apply_matrix(
                grid[lead : lead + out_rows, row_bit, :, side : side + out_cols, col_bit],
                weight[:, across, along],
            )
    return total


def strided_back(grid, grads, weight):
    out_rows = grads.shape[0]
    out_cols = grads.shape[2]
    rows_grad = []
    blocks = [[0.0, 0.0], [0.0, 0.0]]
    for across in range(3):
        lead, row_bit = TAPS[across]
        cols_grad = []
        for along in range(3):
            side, col_bit = TAPS[along]
            cols_grad.append(
                outer_sum(
                    grid[lead : lead + out_rows, row_bit, :, side : side + out_cols, col_bit], grads
                )
            )
            term = apply_transpose(grads, weight[:, across, along])
            blocks[row_bit][col_bit] = blocks[row_bit][col_bit] + jnp.pad(
                term, ((lead, 1 - lead), (0, 0), (side, 1 - side), (0, 0))
            )
        rows_grad.append(jnp.stack(cols_grad, axis=1))
    weight_grad = jnp.stack(rows_grad, axis=1)
    whole = jnp.stack([jnp.stack(blocks[bit], axis=3) for bit in range(2)], axis=1)
    return (
        weight_grad,
        whole.reshape(2 * out_rows + 2, grads.shape[1], 2 * out_cols + 2, whole.shape[-1]),
    )


def spread_even(term):
    count, views, cols, chans = term.shape
    spaced = jnp.stack([term, jnp.zeros_like(term)], axis=3).reshape(count, views, 2 * cols, chans)
    return jnp.stack([spaced, jnp.zeros_like(spaced)], axis=1).reshape(
        2 * count, views, 2 * cols, chans
    )


def spread_grads(grads):
    partial_sums = jax.tree.map(
        lambda part: part.astype(jnp.float32),
        lax.psum_scatter(shortened(grads), "dp", scatter_dimension=0, tiled=True),
    )
    return jax.tree.map(
        lambda part: part.astype(jnp.float32),
        lax.psum_scatter(shortened(partial_sums), "rows", scatter_dimension=0, tiled=True),
    )


def on_device(
    input_a,
    input_b,
    live_views,
    reduce_one,
    spatial_one,
    expand_one,
    reduce_two,
    spatial_two,
    expand_two,
    shortcut_two,
    gain_narrow,
    bias_narrow,
    gain_spatial,
    bias_spatial,
    gain_widened,
    bias_widened,
    gain_squeeze,
    bias_squeeze,
    gain_strided,
    bias_strided,
    gain_output,
    bias_output,
    gain_shortcut,
    bias_shortcut,
    cotangent_a,
    cotangent_b,
):
    inputs = [input_a, input_b]
    heights = [HA, HB]
    masks = [
        strip_mask(
            live_views, group, inputs[group].shape[0], inputs[group].shape[1], heights[group]
        )
        for group in range(2)
    ]
    halves = [
        strip_mask(
            live_views,
            group,
            inputs[group].shape[0] // 2,
            inputs[group].shape[1],
            (heights[group] + 1) // 2,
        )
        for group in range(2)
    ]
    totals = jnp.sum(live_views, axis=0).astype(jnp.float32)
    full_count = HA * WA * totals[0] + HB * WB * totals[1]
    half_count = (HA + 1) // 2 * ((WA + 1) // 2) * totals[0] + (HB + 1) // 2 * (
        (WB + 1) // 2
    ) * totals[1]
    pre_one = [apply_matrix(value, reduce_one) for value in inputs]
    total, square = shared_sums(pre_one, masks)
    unit_one, scale_one = standardize(pre_one, total, square, full_count)
    act_one = [unit * gain_narrow + bias_narrow for unit in unit_one]
    hidden_one = [(silu(value) * mask).astype(jnp.bfloat16) for value, mask in zip(act_one, masks)]
    beside_all = padded_2(rim_pack(hidden_one), (("rows", 0),), 1)
    above_rows = rim_split(beside_all[0], hidden_one)
    below_rows = rim_split(beside_all[3], hidden_one)
    spatial_pairs = [
        spatial_same(jnp.concatenate([upper[None], value, lower[None]], axis=0), spatial_one)
        for upper, value, lower in zip(above_rows, hidden_one, below_rows)
    ]
    pre_two = [pair[0] for pair in spatial_pairs]
    wide_one = [pair[1] for pair in spatial_pairs]
    total, square = shared_sums(pre_two, masks)
    unit_two, scale_two = standardize(pre_two, total, square, full_count)
    act_two = [unit * gain_spatial + bias_spatial for unit in unit_two]
    hidden_two = [(silu(value) * mask).astype(jnp.bfloat16) for value, mask in zip(act_two, masks)]
    pre_three = [apply_matrix(value, expand_one) for value in hidden_two]
    total, square = shared_sums(pre_three, masks)
    unit_three, scale_three = standardize(pre_three, total, square, full_count)
    sum_one = [
        unit * gain_widened + bias_widened + source.astype(jnp.float32)
        for unit, source in zip(unit_three, inputs)
    ]
    feed = [(silu(value) * mask).astype(jnp.bfloat16) for value, mask in zip(sum_one, masks)]
    pre_four = [apply_matrix(value, reduce_two) for value in feed]
    total, square = shared_sums(pre_four, masks)
    unit_four, scale_four = standardize(pre_four, total, square, full_count)
    act_four = [unit * gain_squeeze + bias_squeeze for unit in unit_four]
    hidden_four = [
        (silu(value) * mask).astype(jnp.bfloat16) for value, mask in zip(act_four, masks)
    ]
    last_rows = jnp.concatenate([value[-1].reshape(-1) for value in hidden_four])
    from_above = rim_split(passed_along(last_rows, "rows", 1), hidden_four)
    grids = [strided_grid(value, upper) for value, upper in zip(hidden_four, from_above)]
    pre_five = [strided_forward(grid, spatial_two) for grid in grids]
    total, square = shared_sums(pre_five, halves)
    unit_five, scale_five = standardize(pre_five, total, square, half_count)
    act_five = [unit * gain_strided + bias_strided for unit in unit_five]
    hidden_five = [
        (silu(value) * mask).astype(jnp.bfloat16) for value, mask in zip(act_five, halves)
    ]
    pre_six = [apply_matrix(value, expand_two) for value in hidden_five]
    short_in = [value[0::2, :, 0::2] for value in feed]
    pre_short = [apply_matrix(value, shortcut_two) for value in short_in]
    total_main, square_main = shared_sums(pre_six, halves)
    total_side, square_side = shared_sums(pre_short, halves)
    unit_six, scale_six = standardize(pre_six, total_main, square_main, half_count)
    unit_short, scale_short = standardize(pre_short, total_side, square_side, half_count)
    sum_two = [
        main * gain_output + bias_output + (side * gain_shortcut + bias_shortcut)
        for main, side in zip(unit_six, unit_short)
    ]
    block_out = [(silu(value) * mask).astype(jnp.bfloat16) for value, mask in zip(sum_two, halves)]
    cotangents = [cotangent_a, cotangent_b]
    slope_two = [
        cotangent.astype(jnp.float32) * mask * silu_slope(value)
        for cotangent, mask, value in zip(cotangents, halves, sum_two)
    ]
    grad_bias_output, grad_gain_output = shared_grads(slope_two, unit_six)
    grad_bias_shortcut, grad_gain_shortcut = shared_grads(slope_two, unit_short)
    grad_pre_six = norm_back(
        slope_two,
        unit_six,
        halves,
        scale_six,
        gain_output,
        grad_bias_output,
        grad_gain_output,
        half_count,
    )
    grad_pre_short = norm_back(
        slope_two,
        unit_short,
        halves,
        scale_short,
        gain_shortcut,
        grad_bias_shortcut,
        grad_gain_shortcut,
        half_count,
    )
    grad_expand_two = outer_sum(hidden_five[0], grad_pre_six[0]) + outer_sum(
        hidden_five[1], grad_pre_six[1]
    )
    grad_shortcut_two = outer_sum(short_in[0], grad_pre_short[0]) + outer_sum(
        short_in[1], grad_pre_short[1]
    )
    slope_five = [
        apply_transpose(grad, expand_two) * mask * silu_slope(value)
        for grad, mask, value in zip(grad_pre_six, halves, act_five)
    ]
    grad_bias_strided, grad_gain_strided = shared_grads(slope_five, unit_five)
    grad_pre_five = norm_back(
        slope_five,
        unit_five,
        halves,
        scale_five,
        gain_strided,
        grad_bias_strided,
        grad_gain_strided,
        half_count,
    )
    strided_pairs = [
        strided_back(grid, grad, spatial_two) for grid, grad in zip(grids, grad_pre_five)
    ]
    grad_spatial_two = strided_pairs[0][0] + strided_pairs[1][0]
    wholes = [pair[1] for pair in strided_pairs]
    widths = [value.shape[2] for value in hidden_four]
    sent_up = jnp.concatenate(
        [whole[0, :, 1 : width + 1].reshape(-1) for whole, width in zip(wholes, widths)]
    )
    from_below = rim_split(
        passed_along(sent_up.astype(jnp.bfloat16), "rows", -1).astype(sent_up.dtype), hidden_four
    )
    grad_four = []
    for whole, width, extra, value in zip(wholes, widths, from_below, hidden_four):
        local = whole[1 : value.shape[0] + 1, :, 1 : width + 1]
        grad_four.append(local.at[-1].add(extra))
    slope_four = [
        grad * mask * silu_slope(value) for grad, mask, value in zip(grad_four, masks, act_four)
    ]
    grad_bias_squeeze, grad_gain_squeeze = shared_grads(slope_four, unit_four)
    grad_pre_four = norm_back(
        slope_four,
        unit_four,
        masks,
        scale_four,
        gain_squeeze,
        grad_bias_squeeze,
        grad_gain_squeeze,
        full_count,
    )
    grad_reduce_two = outer_sum(feed[0], grad_pre_four[0]) + outer_sum(feed[1], grad_pre_four[1])
    grad_feed = [
        apply_transpose(grad, reduce_two) + spread_even(apply_transpose(side, shortcut_two))
        for grad, side in zip(grad_pre_four, grad_pre_short)
    ]
    second_block = spread_grads(
        (grad_reduce_two, grad_spatial_two, grad_expand_two, grad_shortcut_two)
    )
    slope_three = [
        grad * mask * silu_slope(value) for grad, mask, value in zip(grad_feed, masks, sum_one)
    ]
    grad_bias_widened, grad_gain_widened = shared_grads(slope_three, unit_three)
    grad_pre_three = norm_back(
        slope_three,
        unit_three,
        masks,
        scale_three,
        gain_widened,
        grad_bias_widened,
        grad_gain_widened,
        full_count,
    )
    grad_expand_one = outer_sum(hidden_two[0], grad_pre_three[0]) + outer_sum(
        hidden_two[1], grad_pre_three[1]
    )
    slope_spatial = [
        apply_transpose(grad, expand_one) * mask * silu_slope(value)
        for grad, mask, value in zip(grad_pre_three, masks, act_two)
    ]
    grad_bias_spatial, grad_gain_spatial = shared_grads(slope_spatial, unit_two)
    grad_pre_two = norm_back(
        slope_spatial,
        unit_two,
        masks,
        scale_two,
        gain_spatial,
        grad_bias_spatial,
        grad_gain_spatial,
        full_count,
    )
    same_pairs = [
        spatial_same_back(wide, grad, spatial_one) for wide, grad in zip(wide_one, grad_pre_two)
    ]
    grad_spatial_one = same_pairs[0][0] + same_pairs[1][0]
    backs = [pair[1] for pair in same_pairs]
    returned = padded_2(rim_pack(backs).astype(jnp.bfloat16), (("rows", 0),), 1).astype(jnp.float32)
    from_upper = rim_split(returned[0], hidden_one)
    from_lower = rim_split(returned[3], hidden_one)
    grad_one = [
        back[1:-1].at[0].add(upper).at[-1].add(lower)
        for back, upper, lower in zip(backs, from_upper, from_lower)
    ]
    slope_narrow = [
        grad * mask * silu_slope(value) for grad, mask, value in zip(grad_one, masks, act_one)
    ]
    grad_bias_narrow, grad_gain_narrow = shared_grads(slope_narrow, unit_one)
    grad_pre_one = norm_back(
        slope_narrow,
        unit_one,
        masks,
        scale_one,
        gain_narrow,
        grad_bias_narrow,
        grad_gain_narrow,
        full_count,
    )
    grad_reduce_one = outer_sum(inputs[0], grad_pre_one[0]) + outer_sum(inputs[1], grad_pre_one[1])
    grad_inputs = [
        (slope + apply_transpose(grad, reduce_one)).astype(jnp.bfloat16)
        for slope, grad in zip(slope_three, grad_pre_one)
    ]
    first_block = spread_grads((grad_reduce_one, grad_spatial_one, grad_expand_one))
    return (
        block_out[0],
        block_out[1],
        grad_inputs[0],
        grad_inputs[1],
        first_block[0],
        first_block[1],
        first_block[2],
        second_block[0],
        second_block[1],
        second_block[2],
        second_block[3],
        grad_gain_narrow,
        grad_bias_narrow,
        grad_gain_spatial,
        grad_bias_spatial,
        grad_gain_widened,
        grad_bias_widened,
        grad_gain_squeeze,
        grad_bias_squeeze,
        grad_gain_strided,
        grad_bias_strided,
        grad_gain_output,
        grad_bias_output,
        grad_gain_shortcut,
        grad_bias_shortcut,
    )


def solution(mesh):
    placed = (
        P("rows", "dp", None, None),
        P("rows", "dp", None, None),
        P(),
        P(),
        P(),
        P(),
        P(),
        P(),
        P(),
        P(),
        P(),
        P(),
        P(),
        P(),
        P(),
        P(),
        P(),
        P(),
        P(),
        P(),
        P(),
        P(),
        P(),
        P(),
        P("rows", "dp", None, None),
        P("rows", "dp", None, None),
    )
    return jax.shard_map(
        on_device,
        mesh=mesh,
        in_specs=placed,
        out_specs=(
            P("rows", "dp", None, None),
            P("rows", "dp", None, None),
            P("rows", "dp", None, None),
            P("rows", "dp", None, None),
            P(("dp", "rows"), None),
            P(("dp", "rows"), None, None, None),
            P(("dp", "rows"), None),
            P(("dp", "rows"), None),
            P(("dp", "rows"), None, None, None),
            P(("dp", "rows"), None),
            P(("dp", "rows"), None),
            P(),
            P(),
            P(),
            P(),
            P(),
            P(),
            P(),
            P(),
            P(),
            P(),
            P(),
            P(),
            P(),
            P(),
        ),
        check_vma=False,
    )
```

profile of v0, /device:TPU:0, one launch (start us, length us, event | category | flops | bytes accessed | tf_op | source)
XLA Modules:
  0.0 1367.3 jit_solution(1175480465734896758)
XLA Ops:
  14.7 42.0 %all-reduce.55 = (f32[256]{0:T(256)S(1)}, f32[256]{0:T(256)S(1)}) all-reduce(f32[256]{0:T(256)S(1)} %add.779, f32[256]{0:T(256)S(1)} %add.782), channel_id=1, replica_groups=mesh['dp'=8,'rows'=4] {'dp','rows'}, use_global_device_ids=true, to_apply=%region_4.5 | all-reduce | flops 512 | bytes 4096 | tf_op jit(solution)/shard_map/psum | solution.py:95
  86.6 40.2 %all-reduce.54 = (f32[256]{0:T(256)S(1)}, f32[256]{0:T(256)S(1)}) all-reduce(f32[256]{0:T(256)S(1)} %add.806, f32[256]{0:T(256)S(1)} %add.807), channel_id=1, replica_groups=mesh['dp'=8,'rows'=4] {'dp','rows'}, use_global_device_ids=true, to_apply=%region_11.12 | all-reduce | flops 512 | bytes 4096 | tf_op jit(solution)/shard_map/psum | solution.py:95
  132.5 40.8 %all-reduce.53 = (f32[1024]{0:T(1024)}, f32[1024]{0:T(1024)}) all-reduce(f32[1024]{0:T(1024)} %add.815, f32[1024]{0:T(1024)} %add.816), channel_id=1, replica_groups=mesh['dp'=8,'rows'=4] {'dp','rows'}, use_global_device_ids=true, to_apply=%region_17.18 | all-reduce | flops 2048 | bytes 16384 | tf_op jit(solution)/shard_map/psum | solution.py:95
  187.2 40.5 %all-reduce.52 = (f32[512]{0:T(512)S(1)}, f32[512]{0:T(512)S(1)}) all-reduce(f32[512]{0:T(512)S(1)} %add.828, f32[512]{0:T(512)S(1)} %add.827), channel_id=1, replica_groups=mesh['dp'=8,'rows'=4] {'dp','rows'}, use_global_device_ids=true, to_apply=%region_26.27 | all-reduce | flops 1024 | bytes 8192 | tf_op jit(solution)/shard_map/psum | solution.py:95
  266.2 40.9 %all-reduce.51 = (f32[512]{0:T(512)S(1)}, f32[512]{0:T(512)S(1)}) all-reduce(f32[512]{0:T(512)S(1)} %add.857, f32[512]{0:T(512)S(1)} %add.854), channel_id=1, replica_groups=mesh['dp'=8,'rows'=4] {'dp','rows'}, use_global_device_ids=true, to_apply=%region_32.33 | all-reduce | flops 1024 | bytes 8192 | tf_op jit(solution)/shard_map/psum | solution.py:95
  313.1 40.6 %all-reduce.50 = (f32[2048]{0:T(1024)S(1)}, f32[2048]{0:T(1024)S(1)}, f32[2048]{0:T(1024)S(1)}, f32[2048]{0:T(1024)S(1)}) all-reduce(f32[2048]{0:T(1024)S(1)} %add.871, f32[2048]{0:T(1024)S(1)} %add.870, f32[2048]{0:T(1024)S(1)} %add.866, f32[2048]{0:T(1024)S(1)} %add.865), channel_id=1, replica_groups=mesh['dp'=8,'rows'=4] {'dp','rows'}, use_global_device_ids=true, to_apply=%region_44.45 | all-reduce | flops 8192 | bytes 65536 | tf_op jit(solution)/shard_map/psum | solution.py:95
  364.2 40.2 %all-reduce.49 = (f32[2048]{0:T(1024)}, f32[2048]{0:T(1024)}) all-reduce(f32[2048]{0:T(1024)} %add.886, f32[2048]{0:T(1024)} %add.885), channel_id=1, replica_groups=mesh['dp'=8,'rows'=4] {'dp','rows'}, use_global_device_ids=true, to_apply=%region_50.51 | all-reduce | flops 4096 | bytes 32768 | tf_op jit(solution)/shard_map/psum | solution.py:115
  411.6 41.0 %all-reduce.48 = (f32[512]{0:T(512)S(1)}, f32[512]{0:T(512)S(1)}) all-reduce(f32[512]{0:T(512)S(1)} %add.890, f32[512]{0:T(512)S(1)} %add.889), channel_id=1, replica_groups=mesh['dp'=8,'rows'=4] {'dp','rows'}, use_global_device_ids=true, to_apply=%region_56.57 | all-reduce | flops 1024 | bytes 8192 | tf_op jit(solution)/shard_map/psum | solution.py:115
  495.8 41.6 %all-reduce.47 = (f32[2048]{0:T(1024)S(1)}, f32[512]{0:T(512)S(1)}, f32[512]{0:T(512)}) all-reduce(f32[2048]{0:T(1024)S(1)} %add.907, f32[512]{0:T(512)S(1)} %add.906, f32[512]{0:T(512)S(1)} %add.905), channel_id=1, replica_groups=mesh['dp'=8,'rows'=4] {'dp','rows'}, use_global_device_ids=true, to_apply=%region_65.66 | all-reduce | flops 3072 | bytes 24576 | tf_op jit(solution)/shard_map/psum | solution.py:115
  557.1 40.8 %all-reduce.46 = (f32[1024]{0:T(1024)S(1)}, f32[1024]{0:T(1024)S(1)}) all-reduce(f32[1024]{0:T(1024)S(1)} %add.913, f32[1024]{0:T(1024)S(1)} %add.912), channel_id=1, replica_groups=mesh['dp'=8,'rows'=4] {'dp','rows'}, use_global_device_ids=true, to_apply=%region_71.72 | all-reduce | flops 2048 | bytes 16384 | tf_op jit(solution)/shard_map/psum | solution.py:115
  604.4 39.9 %all-reduce.45 = (f32[256]{0:T(256)S(1)}, f32[256]{0:T(256)S(1)}) all-reduce(f32[256]{0:T(256)S(1)} %add.917, f32[256]{0:T(256)S(1)} %add.916), channel_id=1, replica_groups=mesh['dp'=8,'rows'=4] {'dp','rows'}, use_global_device_ids=true, to_apply=%region_77.78 | all-reduce | flops 512 | bytes 4096 | tf_op jit(solution)/shard_map/psum | solution.py:115
  687.0 41.6 %all-reduce.44 = (f32[256]{0:T(256)S(1)}, f32[256]{0:T(256)S(1)}) all-reduce(f32[256]{0:T(256)S(1)} %add.941, f32[256]{0:T(256)S(1)} %add.940), channel_id=1, replica_groups=mesh['dp'=8,'rows'=4] {'dp','rows'}, use_global_device_ids=true, to_apply=%region_83.84 | all-reduce | flops 512 | bytes 4096 | tf_op jit(solution)/shard_map/psum | solution.py:115
  776.9 27.3 %reduce-scatter.43.cloned.1.call-done = bf16[128,256]{1,0:T(8,128)(2,1)} async-done(((bf16[1024,256]{1,0:T(8,128)(2,1)}), bf16[128,256]{1,0:T(8,128)(2,1)}) %reduce-scatter.43.cloned.1.call-update) | async-done | bytes 65552
  804.3 65.7 %reduce-scatter.27.cloned.1.call-done = bf16[128,512]{1,0:T(8,128)(2,1)} async-done(((bf16[1024,512]{1,0:T(8,128)(2,1)}), bf16[128,512]{1,0:T(8,128)(2,1)}) %reduce-scatter.27.cloned.1.call-update) | async-done | bytes 131088 | tf_op jit(solution)/shard_map/reduce_scatter | solution.py:240
  870.1 67.4 %reduce-scatter.21.cloned.1.call-done = bf16[32,3,3,256]{3,0,2,1:T(8,128)(2,1)} async-done(((bf16[256,3,3,256]{3,0,2,1:T(8,128)(2,1)}), bf16[32,3,3,256]{3,0,2,1:T(8,128)(2,1)}) %reduce-scatter.21.cloned.1.call-update) | async-done | bytes 147472 | tf_op jit(solution)/shard_map/reduce_scatter | solution.py:240
  939.4 68.8 %reduce-scatter.35.cloned.1.call-done = bf16[64,2048]{1,0:T(8,128)(2,1)} async-done(((bf16[512,2048]{1,0:T(8,128)(2,1)}), bf16[64,2048]{1,0:T(8,128)(2,1)}) %reduce-scatter.35.cloned.1.call-update) | async-done | bytes 262160 | tf_op jit(solution)/shard_map/reduce_scatter | solution.py:240
  1008.2 90.8 %reduce-scatter.39.cloned.1.call-done = bf16[128,2048]{1,0:T(8,128)(2,1)} async-done(((bf16[1024,2048]{1,0:T(8,128)(2,1)}), bf16[128,2048]{1,0:T(8,128)(2,1)}) %reduce-scatter.39.cloned.1.call-update) | async-done | bytes 524304 | tf_op jit(solution)/shard_map/reduce_scatter | solution.py:240
  1099.3 98.9 %reduce-scatter.31.cloned.1.call-done = bf16[64,3,3,512]{3,0,2,1:T(8,128)(2,1)} async-done(((bf16[512,3,3,512]{3,0,2,1:T(8,128)(2,1)}), bf16[64,3,3,512]{3,0,2,1:T(8,128)(2,1)}) %reduce-scatter.31.cloned.1.call-update) | async-done | bytes 589840 | tf_op jit(solution)/shard_map/reduce_scatter | solution.py:240
  1221.2 20.7 %reduce-scatter.45.cloned.1.call-done = bf16[32,256]{1,0:T(8,128)(2,1)} async-done(((bf16[128,256]{1,0:T(8,128)(2,1)}), bf16[32,256]{1,0:T(8,128)(2,1)}) %reduce-scatter.45.cloned.1.call-update) | async-done | bytes 16400
  1243.5 20.3 %reduce-scatter.29.cloned.1.call-done = bf16[32,512]{1,0:T(8,128)(2,1)} async-done(((bf16[128,512]{1,0:T(8,128)(2,1)}), bf16[32,512]{1,0:T(8,128)(2,1)}) %reduce-scatter.29.cloned.1.call-update) | async-done | bytes 32784 | tf_op jit(solution)/shard_map/reduce_scatter | solution.py:244
  1265.2 21.5 %reduce-scatter.47.cloned.1.call-done = bf16[8,2304]{1,0:T(8,128)(2,1)} async-done(((bf16[32,2304]{1,0:T(8,128)(2,1)}), bf16[8,2304]{1,0:T(8,128)(2,1)}) %reduce-scatter.47.cloned.1.call-update) | async-done | bytes 36880
  1288.0 21.1 %reduce-scatter.37.cloned.1.call-done = bf16[16,2048]{1,0:T(8,128)(2,1)} async-done(((bf16[64,2048]{1,0:T(8,128)(2,1)}), bf16[16,2048]{1,0:T(8,128)(2,1)}) %reduce-scatter.37.cloned.1.call-update) | async-done | bytes 65552 | tf_op jit(solution)/shard_map/reduce_scatter | solution.py:244
  1310.7 22.7 %reduce-scatter.41.cloned.1.call-done = bf16[32,2048]{1,0:T(8,128)(2,1)} async-done(((bf16[128,2048]{1,0:T(8,128)(2,1)}), bf16[32,2048]{1,0:T(8,128)(2,1)}) %reduce-scatter.41.cloned.1.call-update) | async-done | bytes 131088 | tf_op jit(solution)/shard_map/reduce_scatter | solution.py:244
  1335.0 23.0 %reduce-scatter.33.cloned.1.call-done = bf16[16,3,3,512]{3,0,2,1:T(8,128)(2,1)} async-done(((bf16[64,3,3,512]{3,0,2,1:T(8,128)(2,1)}), bf16[16,3,3,512]{3,0,2,1:T(8,128)(2,1)}) %reduce-scatter.33.cloned.1.call-update) | async-done | bytes 147472 | tf_op jit(solution)/shard_map/reduce_scatter | solution.py:244
  (973 shorter events, 307.8 us)
Async XLA Ops:
  7.2 301.1 %copy-start = (bf16[512,2048]{1,0:T(8,128)(2,1)S(1)}, bf16[512,2048]{1,0:T(8,128)(2,1)}, u32[]{:S(2)}) copy-start(bf16[512,2048]{1,0:T(8,128)(2,1)} %param.46) | copy-start | bytes 6291460
  7.2 769.0 %reduce-scatter.23.cloned.1.call-start = ((), (), s32[]{:S(2)}) async-start(), calls=%async_computation.15 | async-start | bytes 589824 | tf_op jit(solution)/shard_map/reduce_scatter | solution.py:240
  59.9 9.4 collective-permute-start.1
  61.2 8.3 collective-permute-start
  231.6 6.8 collective-permute-start.2
  484.4 4.1 collective-permute-start.3
  671.3 7.6 collective-permute-start.5
  672.6 6.3 collective-permute-start.4
  677.8 126.5 %reduce-scatter.43.cloned.1.call-start = ((), (), s32[]{:S(2)}) async-start(), calls=%async_computation.25 | async-start | bytes 589824
  734.5 135.5 %reduce-scatter.27.cloned.1.call-start = ((), (), s32[]{:S(2)}) async-start(), calls=%async_computation.17 | async-start | bytes 1179648 | tf_op jit(solution)/shard_map/reduce_scatter | solution.py:240
  738.5 199.0 %reduce-scatter.21.cloned.1.call-start = ((), (), s32[]{:S(2)}) async-start(), calls=%async_computation.14 | async-start | bytes 1327104 | tf_op jit(solution)/shard_map/reduce_scatter | solution.py:240
  744.7 263.4 %reduce-scatter.35.cloned.1.call-start = ((), (), s32[]{:S(2)}) async-start(), calls=%async_computation.21 | async-start | bytes 2359296 | tf_op jit(solution)/shard_map/reduce_scatter | solution.py:240
  749.0 350.0 %reduce-scatter.39.cloned.1.call-start = ((), (), s32[]{:S(2)}) async-start(), calls=%async_computation.23 | async-start | bytes 4718592 | tf_op jit(solution)/shard_map/reduce_scatter | solution.py:240
  755.7 442.5 %reduce-scatter.31.cloned.1.call-start = ((), (), s32[]{:S(2)}) async-start(), calls=%async_computation.19 | async-start | bytes 5308416 | tf_op jit(solution)/shard_map/reduce_scatter | solution.py:240
  776.1 422.2 %copy-start.81 = (bf16[2,4,7,2048]{3,2,1,0:T(8,128)(2,1)S(1)}, bf16[2,4,7,2048]{3,2,1,0:T(8,128)(2,1)}, u32[]{:S(2)}) copy-start(bf16[2,4,7,2048]{3,2,1,0:T(8,128)(2,1)} %get-tuple-element.293) | copy-start | bytes 688132
  776.1 443.8 %reduce-scatter.25.cloned.1.call-start = ((), (), s32[]{:S(2)}) async-start(), calls=%async_computation.16 | async-start | bytes 81920 | tf_op jit(solution)/shard_map/reduce_scatter | solution.py:244
  776.9 465.1 %reduce-scatter.45.cloned.1.call-start = ((), (), s32[]{:S(2)}) async-start(), calls=%async_computation.26 | async-start | bytes 81920
  804.3 459.5 %reduce-scatter.29.cloned.1.call-start = ((), (), s32[]{:S(2)}) async-start(), calls=%async_computation.18 | async-start | bytes 163840 | tf_op jit(solution)/shard_map/reduce_scatter | solution.py:244
  870.0 329.2 %copy-start.39 = (bf16[2,12,5,2048]{3,1,2,0:T(8,128)(2,1)S(1)}, bf16[2,12,5,2048]{3,1,2,0:T(8,128)(2,1)}, u32[]{:S(2)}) copy-start(bf16[2,12,5,2048]{3,1,2,0:T(8,128)(2,1)} %get-tuple-element.283) | copy-start | bytes 1474564
  870.0 416.6 %reduce-scatter.47.cloned.1.call-start = ((), (), s32[]{:S(2)}) async-start(), calls=%async_computation.27 | async-start | bytes 184320
  939.3 369.9 %reduce-scatter.37.cloned.1.call-start = ((), (), s32[]{:S(2)}) async-start(), calls=%async_computation.22 | async-start | bytes 327680 | tf_op jit(solution)/shard_map/reduce_scatter | solution.py:244
  1008.2 325.2 %reduce-scatter.41.cloned.1.call-start = ((), (), s32[]{:S(2)}) async-start(), calls=%async_computation.24 | async-start | bytes 655360 | tf_op jit(solution)/shard_map/reduce_scatter | solution.py:244
  1099.0 259.0 %reduce-scatter.33.cloned.1.call-start = ((), (), s32[]{:S(2)}) async-start(), calls=%async_computation.20 | async-start | bytes 737280 | tf_op jit(solution)/shard_map/reduce_scatter | solution.py:244
  1202.9 157.3 %copy-start.1 = (bf16[512,2048]{1,0:T(8,128)(2,1)S(1)}, bf16[512,2048]{1,0:T(8,128)(2,1)}, u32[]{:S(2)}) copy-start(bf16[512,2048]{1,0:T(8,128)(2,1)} %param.46) | copy-start | bytes 6291460
  (263 other events, 2469.0 us)
Sparse Core Ops, SparseCore 0:
  677.8 61.6 reduce-scatter.22
  743.2 60.9 reduce-scatter.42
  807.6 62.2 reduce-scatter.26
  873.6 63.7 reduce-scatter.20
  941.2 66.8 reduce-scatter.34
  1012.1 86.8 reduce-scatter.38
  1102.6 95.5 reduce-scatter.30
  1200.7 19.1 reduce-scatter.24
  1222.4 19.4 reduce-scatter.44
  1244.2 19.5 reduce-scatter.28
  1266.9 19.6 reduce-scatter.46
  1289.1 20.0 reduce-scatter.36
  1311.7 21.6 reduce-scatter.40
  1335.9 22.0 reduce-scatter.32
where the time goes:
time: 1380 us; the launch traced here: 1370 us
  waiting for transfers between devices  564 us (41%)
  blocking collectives  490 us (36%)
  matrix products  127 us (9%)
  other arithmetic  76.6 us (6%)
  local copies, waits for them, and re-layouts  74.4 us (5%)
  between operations  21.3 us (2%)
    reduce_scatter x6, waiting for transfers between devices, spread_grads(): lax.psum_scatter(shortened(grads), 'dp', scatter_dimension=0, tiled=True)  391 us
    psum x6, blocking collectives, shared_grads(): return lax.psum((first, second), ('dp', 'rows'))  245 us
    psum x6, blocking collectives, shared_sums(): return lax.psum((total, square), ('dp', 'rows'))  245 us
    reduce_scatter x5, waiting for transfers between devices, spread_grads(): lax.psum_scatter(shortened(partial_sums), 'rows', scatter_dimension=0, ti...  102 us
    unnamed x17, waiting for transfers between devices  70.4 us
    dot_general x46, matrix products, apply_matrix(): out = jnp.dot(flat, matrix, preferred_element_type=jnp.float32)  42.4 us
    dot_general x41, matrix products, apply_transpose(): lax.dot_general(flat, matrix, (((1,), (1,)), ((), ())), preferred_element...  41.1 us
    dot_general x46, matrix products, outer_sum(): lax.dot_general(acts.reshape(-1, acts.shape[-1]), grads.reshape(-1, grads...  39.8 us
  transfers between devices with their start and end apart: 20, of which 13 were waited for; matrix products, arithmetic and copies ran while one was open for 6% of the time, Pallas kernels for 0%

commit v1 on v0

--- a/solution.py
+++ b/solution.py
@@ -1,7 +1,14 @@
+import functools
+import math
+
 import jax
 import jax.numpy as jnp
 from jax import lax
+from jax.experimental import pallas as pl
+from jax.experimental.pallas import tpu as pltpu
 from jax.sharding import PartitionSpec as P
+
+MESH = pl.DeviceIdType.MESH
 
 HA = 14
 WA = 14
@@ -11,6 +18,86 @@
 
 EPS = 1e-05
 TAPS = ((0, 0), (0, 1), (1, 0))
+
+def greet_all(spans):
+    d_size, r_size = spans
+    total = d_size * r_size
+    barrier = pltpu.get_barrier_semaphore()
+    me = lax.axis_index("dp") * r_size + lax.axis_index("rows")
+
+    def greet(step, carry):
+        other = lax.rem(me + step, total)
+        pl.semaphore_signal(
+            barrier,
+            inc=1,
+            device_id=(other // r_size, lax.rem(other, r_size)),
+            device_id_type=MESH,
+        )
+        return carry
+
+    lax.fori_loop(1, total, greet, 0)
+    pl.semaphore_wait(barrier, total - 1)
+
+
+def sum_kernel(spans, in_ref, out_ref, near, mid, far, near_send, near_recv, far_send, far_recv):
+    d_size, r_size = spans
+    d, r = lax.axis_index("dp"), lax.axis_index("rows")
+    greet_all(spans)
+    for step in range(1, r_size):
+        pltpu.make_async_remote_copy(
+            in_ref,
+            near.at[r],
+            near_send,
+            near_recv,
+            device_id=(d, lax.rem(r + step, r_size)),
+            device_id_type=MESH,
+        ).start()
+    near[r] = in_ref[...]
+    several = near.at[0 : r_size - 1]
+    pltpu.make_async_copy(several, several, near_recv).wait()
+    mid[...] = jnp.sum(near[...], axis=0)
+    for step in range(1, d_size):
+        pltpu.make_async_remote_copy(
+            mid,
+            far.at[d],
+            far_send,
+            far_recv,
+            device_id=(lax.rem(d + step, d_size), r),
+            device_id_type=MESH,
+        ).start()
+    far[d] = mid[...]
+    many = far.at[0 : d_size - 1]
+    pltpu.make_async_copy(many, many, far_recv).wait()
+    pltpu.make_async_copy(several, several, near_send).wait()
+    pltpu.make_async_copy(many, many, far_send).wait()
+    out_ref[...] = jnp.sum(far[...], axis=0)
+
+
+def summed(values):
+    spans = (lax.axis_size("dp"), lax.axis_size("rows"))
+    flat = jnp.stack(values)
+    dma = pltpu.SemaphoreType.DMA
+    out = pl.pallas_call(
+        functools.partial(sum_kernel, spans),
+        out_shape=jax.ShapeDtypeStruct(flat.shape, flat.dtype),
+        in_specs=[pl.BlockSpec(memory_space=pltpu.VMEM)],
+        out_specs=pl.BlockSpec(memory_space=pltpu.VMEM),
+        scratch_shapes=[
+            pltpu.VMEM((spans[1],) + flat.shape, flat.dtype),
+            pltpu.VMEM(flat.shape, flat.dtype),
+            pltpu.VMEM((spans[0],) + flat.shape, flat.dtype),
+            dma,
+            dma,
+            dma,
+            dma,
+        ],
+        compiler_params=pltpu.CompilerParams(
+            collective_id=flat.size // 512,
+            has_side_effects=True,
+            vmem_limit_bytes=32 * 2**20,
+        ),
+    )(flat)
+    return tuple(out[i] for i in range(len(values)))
 
 
 def shortened(value):
@@ -92,7 +179,7 @@
 
 def shared_sums(parts, masks):
     total, square = masked_sums(parts, masks)
-    return lax.psum((total, square), ("dp", "rows"))
+    return summed((total, square))
 
 
 def standardize(parts, total, square, count):
@@ -112,7 +199,7 @@
 
 def shared_grads(slopes, normed):
     first, second = slope_sums(slopes, normed)
-    return lax.psum((first, second), ("dp", "rows"))
+    return summed((first, second))
 
 
 def norm_back(slopes, normed, masks, scale, gain, first, second, count):
@@ -342,8 +429,9 @@
     pre_six = [apply_matrix(value, expand_two) for value in hidden_five]
     short_in = [value[0::2, :, 0::2] for value in feed]
     pre_short = [apply_matrix(value, shortcut_two) for value in short_in]
-    total_main, square_main = shared_sums(pre_six, halves)
-    total_side, square_side = shared_sums(pre_short, halves)
+    total_main, square_main, total_side, square_side = summed(
+        masked_sums(pre_six, halves) + masked_sums(pre_short, halves)
+    )
     unit_six, scale_six = standardize(pre_six, total_main, square_main, half_count)
     unit_short, scale_short = standardize(pre_short, total_side, square_side, half_count)
     sum_two = [
@@ -356,8 +444,10 @@
         cotangent.astype(jnp.float32) * mask * silu_slope(value)
         for cotangent, mask, value in zip(cotangents, halves, sum_two)
     ]
-    grad_bias_output, grad_gain_output = shared_grads(slope_two, unit_six)
-    grad_bias_shortcut, grad_gain_shortcut = shared_grads(slope_two, unit_short)
+    first, second = slope_sums(slope_two, unit_six)
+    third = slope_sums(slope_two, unit_short)[1]
+    grad_bias_output, grad_gain_output, grad_gain_shortcut = summed((first, second, third))
+    grad_bias_shortcut = grad_bias_output
     grad_pre_six = norm_back(
         slope_two,
         unit_six,

time: 1380 us -> 1000 us (0.72)
  blocking collectives: 490 us -> 0 us
  Pallas kernels: 0 us -> 133 us
  waiting for transfers between devices: 564 us -> 597 us
  matrix products: 127 us -> 105 us
  other arithmetic: 76.6 us -> 57.7 us
    psum x12 -> x0, blocking collectives: 490 us -> none  [the longest x6 245 us: shared_grads(): return lax.psum((first, second), ('dp', 'rows'))]
    pallas_call x0 -> x12, Pallas kernels: none -> 133 us  [summed(): pl.pallas_call(functools.partial(sum_kernel, spans), out_shape=jax.ShapeD...]
    unnamed x17, waiting for transfers between devices: 70.4 us -> 103 us
    dot_general x41, matrix products: 41.1 us -> 26.4 us  [apply_transpose(): lax.dot_general(flat, matrix, (((1,), (1,)), ((), ())), preferred_element...]
    unnamed x558 -> x450, local copies, waits for them, and re-layouts: 38.2 us -> 38.4 us
  transfers between devices with their start and end apart: 20 -> 20, of which waited for: 13 -> 13; matrix products, arithmetic and copies ran while one was open for 6% -> 9% of each run, Pallas kernels for 0% -> 1%
where the time goes in v1:
time: 1000 us; the launch traced here: 998 us
  waiting for transfers between devices  597 us (60%)
  Pallas kernels  133 us (13%)
  matrix products  105 us (10%)
  local copies, waits for them, and re-layouts  70.4 us (7%)
  other arithmetic  57.7 us (6%)
  between operations  21 us (2%)
  starting transfers between devices  13.4 us (1%)
    reduce_scatter x6, waiting for transfers between devices, spread_grads(): lax.psum_scatter(shortened(grads), 'dp', scatter_dimension=0, tiled=True)  392 us
    pallas_call x12, Pallas kernels, summed(): pl.pallas_call(functools.partial(sum_kernel, spans), out_shape=jax.ShapeD...  133 us
    unnamed x17, waiting for transfers between devices  103 us
    reduce_scatter x5, waiting for transfers between devices, spread_grads(): lax.psum_scatter(shortened(partial_sums), 'rows', scatter_dimension=0, ti...  102 us
    dot_general x46, matrix products, outer_sum(): lax.dot_general(acts.reshape(-1, acts.shape[-1]), grads.reshape(-1, grads...  39.9 us
    unnamed x450, local copies, waits for them, and re-layouts  38.4 us
    dot_general x46, matrix products, apply_matrix(): out = jnp.dot(flat, matrix, preferred_element_type=jnp.float32)  35.2 us
    dot_general x41, matrix products, apply_transpose(): lax.dot_general(flat, matrix, (((1,), (1,)), ((), ())), preferred_element...  26.4 us
  transfers between devices with their start and end apart: 20, of which 13 were waited for; matrix products, arithmetic and copies ran while one was open for 9% of the time, Pallas kernels for 1%

profile of v1, /device:TPU:0, one launch (start us, length us, event | category | flops | bytes accessed | tf_op | source)
XLA Modules:
  0.0 997.7 jit_solution(6519536224894538628)
XLA Ops:
  14.1 11.9 %shard_map.441 = f32[2,256]{1,0:T(2,128)S(1)} custom-call(f32[2,256]{1,0:T(2,128)S(1)} %pad_maximum_fusion.29.in_ref), custom_call_target="tpu_custom_call" | custom-call | tf_op jit(solution)/shard_map/pallas_call | solution.py:80
  54.8 10.7 %shard_map.442 = f32[2,256]{1,0:T(2,128)S(1)} custom-call(f32[2,256]{1,0:T(2,128)S(1)} %pad_maximum_fusion.30.in_ref), custom_call_target="tpu_custom_call" | custom-call | tf_op jit(solution)/shard_map/pallas_call | solution.py:80
  68.9 10.2 %shard_map.443 = f32[2,1024]{1,0:T(2,128)S(1)} custom-call(f32[2,1024]{1,0:T(2,128)S(1)} %pad_maximum_fusion.23.in_ref), custom_call_target="tpu_custom_call" | custom-call | tf_op jit(solution)/shard_map/pallas_call | solution.py:80
  87.3 10.1 %shard_map.444 = f32[2,512]{1,0:T(2,128)S(1)} custom-call(f32[2,512]{1,0:T(2,128)S(1)} %pad_maximum_fusion.25.in_ref), custom_call_target="tpu_custom_call" | custom-call | tf_op jit(solution)/shard_map/pallas_call | solution.py:80
  133.7 10.9 %shard_map.445 = f32[2,512]{1,0:T(2,128)S(1)} custom-call(f32[2,512]{1,0:T(2,128)S(1)} %pad_maximum_fusion.26.in_ref), custom_call_target="tpu_custom_call" | custom-call | tf_op jit(solution)/shard_map/pallas_call | solution.py:80
  147.0 12.7 %shard_map.446 = f32[4,2048]{1,0:T(4,128)S(1)} custom-call(f32[4,2048]{1,0:T(4,128)S(1)} %pad_maximum_fusion.21.in_ref), custom_call_target="tpu_custom_call" | custom-call | tf_op jit(solution)/shard_map/pallas_call | solution.py:80
  163.4 14.2 %shard_map.447 = f32[3,2048]{1,0:T(4,128)S(1)} custom-call(f32[3,2048]{1,0:T(4,128)S(1)} %pad_maximum_fusion.22.in_ref), custom_call_target="tpu_custom_call" | custom-call | tf_op jit(solution)/shard_map/pallas_call | solution.py:80
  182.6 10.6 %shard_map.448 = f32[2,512]{1,0:T(2,128)S(1)} custom-call(f32[2,512]{1,0:T(2,128)S(1)} %pad_maximum_fusion.27.in_ref), custom_call_target="tpu_custom_call" | custom-call | tf_op jit(solution)/shard_map/pallas_call | solution.py:80
  234.3 11.0 %shard_map.449 = f32[2,512]{1,0:T(2,128)S(1)} custom-call(f32[2,512]{1,0:T(2,128)S(1)} %pad_maximum_fusion.28.in_ref), custom_call_target="tpu_custom_call" | custom-call | tf_op jit(solution)/shard_map/pallas_call | solution.py:80
  253.5 10.2 %shard_map.450 = f32[2,1024]{1,0:T(2,128)S(1)} custom-call(f32[2,1024]{1,0:T(2,128)S(1)} %pad_maximum_fusion.24.in_ref), custom_call_target="tpu_custom_call" | custom-call | tf_op jit(solution)/shard_map/pallas_call | solution.py:80
  318.7 10.6 %shard_map.452 = f32[2,256]{1,0:T(2,128)S(1)} custom-call(f32[2,256]{1,0:T(2,128)S(1)} %pad_maximum_fusion.32.in_ref), custom_call_target="tpu_custom_call" | custom-call | tf_op jit(solution)/shard_map/pallas_call | solution.py:80
  375.5 59.5 %reduce-scatter.43.cloned.1.call-done = bf16[128,256]{1,0:T(8,128)(2,1)} async-done(((bf16[1024,256]{1,0:T(8,128)(2,1)}), bf16[128,256]{1,0:T(8,128)(2,1)}) %reduce-scatter.43.cloned.1.call-update) | async-done | bytes 65552
  435.0 65.9 %reduce-scatter.27.cloned.1.call-done = bf16[128,512]{1,0:T(8,128)(2,1)} async-done(((bf16[1024,512]{1,0:T(8,128)(2,1)}), bf16[128,512]{1,0:T(8,128)(2,1)}) %reduce-scatter.27.cloned.1.call-update) | async-done | bytes 131088 | tf_op jit(solution)/shard_map/reduce_scatter | solution.py:327
  501.0 67.4 %reduce-scatter.21.cloned.1.call-done = bf16[32,3,3,256]{3,0,2,1:T(8,128)(2,1)} async-done(((bf16[256,3,3,256]{3,0,2,1:T(8,128)(2,1)}), bf16[32,3,3,256]{3,0,2,1:T(8,128)(2,1)}) %reduce-scatter.21.cloned.1.call-update) | async-done | bytes 147472 | tf_op jit(solution)/shard_map/reduce_scatter | solution.py:327
  570.3 68.6 %reduce-scatter.35.cloned.1.call-done = bf16[64,2048]{1,0:T(8,128)(2,1)} async-done(((bf16[512,2048]{1,0:T(8,128)(2,1)}), bf16[64,2048]{1,0:T(8,128)(2,1)}) %reduce-scatter.35.cloned.1.call-update) | async-done | bytes 262160 | tf_op jit(solution)/shard_map/reduce_scatter | solution.py:327
  638.9 90.9 %reduce-scatter.39.cloned.1.call-done = bf16[128,2048]{1,0:T(8,128)(2,1)} async-done(((bf16[1024,2048]{1,0:T(8,128)(2,1)}), bf16[128,2048]{1,0:T(8,128)(2,1)}) %reduce-scatter.39.cloned.1.call-update) | async-done | bytes 524304 | tf_op jit(solution)/shard_map/reduce_scatter | solution.py:327
  730.0 99.2 %reduce-scatter.31.cloned.1.call-done = bf16[64,3,3,512]{3,0,2,1:T(8,128)(2,1)} async-done(((bf16[512,3,3,512]{3,0,2,1:T(8,128)(2,1)}), bf16[64,3,3,512]{3,0,2,1:T(8,128)(2,1)}) %reduce-scatter.31.cloned.1.call-update) | async-done | bytes 589840 | tf_op jit(solution)/shard_map/reduce_scatter | solution.py:327
  835.5 15.2 %reduce-scatter.25.cloned.1.call-done = bf16[8,1024]{1,0:T(8,128)(2,1)} async-done(((bf16[32,1024]{1,0:T(8,128)(2,1)}), bf16[8,1024]{1,0:T(8,128)(2,1)}) %reduce-scatter.25.cloned.1.call-update) | async-done | bytes 16400 | tf_op jit(solution)/shard_map/reduce_scatter | solution.py:331
  852.1 20.7 %reduce-scatter.45.cloned.1.call-done = bf16[32,256]{1,0:T(8,128)(2,1)} async-done(((bf16[128,256]{1,0:T(8,128)(2,1)}), bf16[32,256]{1,0:T(8,128)(2,1)}) %reduce-scatter.45.cloned.1.call-update) | async-done | bytes 16400
  874.3 20.4 %reduce-scatter.29.cloned.1.call-done = bf16[32,512]{1,0:T(8,128)(2,1)} async-done(((bf16[128,512]{1,0:T(8,128)(2,1)}), bf16[32,512]{1,0:T(8,128)(2,1)}) %reduce-scatter.29.cloned.1.call-update) | async-done | bytes 32784 | tf_op jit(solution)/shard_map/reduce_scatter | solution.py:331
  896.0 21.4 %reduce-scatter.47.cloned.1.call-done = bf16[8,2304]{1,0:T(8,128)(2,1)} async-done(((bf16[32,2304]{1,0:T(8,128)(2,1)}), bf16[8,2304]{1,0:T(8,128)(2,1)}) %reduce-scatter.47.cloned.1.call-update) | async-done | bytes 36880
  918.9 21.1 %reduce-scatter.37.cloned.1.call-done = bf16[16,2048]{1,0:T(8,128)(2,1)} async-done(((bf16[64,2048]{1,0:T(8,128)(2,1)}), bf16[16,2048]{1,0:T(8,128)(2,1)}) %reduce-scatter.37.cloned.1.call-update) | async-done | bytes 65552 | tf_op jit(solution)/shard_map/reduce_scatter | solution.py:331
  941.5 22.7 %reduce-scatter.41.cloned.1.call-done = bf16[32,2048]{1,0:T(8,128)(2,1)} async-done(((bf16[128,2048]{1,0:T(8,128)(2,1)}), bf16[32,2048]{1,0:T(8,128)(2,1)}) %reduce-scatter.41.cloned.1.call-update) | async-done | bytes 131088 | tf_op jit(solution)/shard_map/reduce_scatter | solution.py:331
  965.8 22.9 %reduce-scatter.33.cloned.1.call-done = bf16[16,3,3,512]{3,0,2,1:T(8,128)(2,1)} async-done(((bf16[64,3,3,512]{3,0,2,1:T(8,128)(2,1)}), bf16[16,3,3,512]{3,0,2,1:T(8,128)(2,1)}) %reduce-scatter.33.cloned.1.call-update) | async-done | bytes 147472 | tf_op jit(solution)/shard_map/reduce_scatter | solution.py:331
  (885 shorter events, 257.8 us)
Async XLA Ops:
  7.2 367.5 %reduce-scatter.23.cloned.1.call-start = ((), (), s32[]{:S(2)}) async-start(), calls=%async_computation.15 | async-start | bytes 589824 | tf_op jit(solution)/shard_map/reduce_scatter | solution.py:327
  31.7 9.7 collective-permute-start.1
  33.0 8.6 collective-permute-start
  99.9 7.1 collective-permute-start.2
  219.5 8.4 collective-permute-start.3
  302.4 8.2 collective-permute-start.5
  303.7 6.9 collective-permute-start.4
  309.6 125.3 %reduce-scatter.43.cloned.1.call-start = ((), (), s32[]{:S(2)}) async-start(), calls=%async_computation.25 | async-start | bytes 589824
  334.6 166.4 %reduce-scatter.27.cloned.1.call-start = ((), (), s32[]{:S(2)}) async-start(), calls=%async_computation.17 | async-start | bytes 1179648 | tf_op jit(solution)/shard_map/reduce_scatter | solution.py:327
  338.5 229.9 %reduce-scatter.21.cloned.1.call-start = ((), (), s32[]{:S(2)}) async-start(), calls=%async_computation.14 | async-start | bytes 1327104 | tf_op jit(solution)/shard_map/reduce_scatter | solution.py:327
  344.7 294.2 %reduce-scatter.35.cloned.1.call-start = ((), (), s32[]{:S(2)}) async-start(), calls=%async_computation.21 | async-start | bytes 2359296 | tf_op jit(solution)/shard_map/reduce_scatter | solution.py:327
  349.0 380.9 %reduce-scatter.39.cloned.1.call-start = ((), (), s32[]{:S(2)}) async-start(), calls=%async_computation.23 | async-start | bytes 4718592 | tf_op jit(solution)/shard_map/reduce_scatter | solution.py:327
  355.7 473.4 %reduce-scatter.31.cloned.1.call-start = ((), (), s32[]{:S(2)}) async-start(), calls=%async_computation.19 | async-start | bytes 5308416 | tf_op jit(solution)/shard_map/reduce_scatter | solution.py:327
  374.6 454.5 %copy-start.67 = (bf16[2,4,7,2048]{3,2,1,0:T(8,128)(2,1)S(1)}, bf16[2,4,7,2048]{3,2,1,0:T(8,128)(2,1)}, u32[]{:S(2)}) copy-start(bf16[2,4,7,2048]{3,2,1,0:T(8,128)(2,1)} %get-tuple-element.256) | copy-start | bytes 688132
  374.7 476.1 %reduce-scatter.25.cloned.1.call-start = ((), (), s32[]{:S(2)}) async-start(), calls=%async_computation.16 | async-start | bytes 81920 | tf_op jit(solution)/shard_map/reduce_scatter | solution.py:331
  375.4 497.3 %reduce-scatter.45.cloned.1.call-start = ((), (), s32[]{:S(2)}) async-start(), calls=%async_computation.26 | async-start | bytes 81920
  435.0 459.7 %reduce-scatter.29.cloned.1.call-start = ((), (), s32[]{:S(2)}) async-start(), calls=%async_computation.18 | async-start | bytes 163840 | tf_op jit(solution)/shard_map/reduce_scatter | solution.py:331
  500.9 329.1 %copy-start.36 = (bf16[2,12,5,2048]{3,1,2,0:T(8,128)(2,1)S(1)}, bf16[2,12,5,2048]{3,1,2,0:T(8,128)(2,1)}, u32[]{:S(2)}) copy-start(bf16[2,12,5,2048]{3,1,2,0:T(8,128)(2,1)} %get-tuple-element.244) | copy-start | bytes 1474564
  500.9 416.5 %reduce-scatter.47.cloned.1.call-start = ((), (), s32[]{:S(2)}) async-start(), calls=%async_computation.27 | async-start | bytes 184320
  570.3 369.7 %reduce-scatter.37.cloned.1.call-start = ((), (), s32[]{:S(2)}) async-start(), calls=%async_computation.22 | async-start | bytes 327680 | tf_op jit(solution)/shard_map/reduce_scatter | solution.py:331
  638.9 325.3 %reduce-scatter.41.cloned.1.call-start = ((), (), s32[]{:S(2)}) async-start(), calls=%async_computation.24 | async-start | bytes 655360 | tf_op jit(solution)/shard_map/reduce_scatter | solution.py:331
  729.9 258.8 %reduce-scatter.33.cloned.1.call-start = ((), (), s32[]{:S(2)}) async-start(), calls=%async_computation.20 | async-start | bytes 737280 | tf_op jit(solution)/shard_map/reduce_scatter | solution.py:331
  833.8 156.6 %copy-start.153 = (f32[1,2048]{1,0:T(1,128)S(1)}, f32[1,2048]{1,0:T(1,128)}, u32[]{:S(2)}) copy-start(f32[1,2048]{1,0:T(1,128)} %copy-done.152) | copy-start | bytes 24580
  833.8 157.2 %copy-start.1 = (bf16[512,2048]{1,0:T(8,128)(2,1)S(1)}, bf16[512,2048]{1,0:T(8,128)(2,1)}, u32[]{:S(2)}) copy-start(bf16[512,2048]{1,0:T(8,128)(2,1)} %param.46) | copy-start | bytes 6291460
  (209 other events, 1715.1 us)
Sparse Core Ops, SparseCore 0:
  309.7 60.4 reduce-scatter.22
  374.0 60.9 reduce-scatter.42
  438.4 62.4 reduce-scatter.26
  504.6 63.7 reduce-scatter.20
  572.2 66.6 reduce-scatter.34
  642.8 87.0 reduce-scatter.38
  733.5 95.5 reduce-scatter.30
  831.5 19.1 reduce-scatter.24
  853.3 19.4 reduce-scatter.44
  875.0 19.5 reduce-scatter.28
  897.8 19.6 reduce-scatter.46
  919.9 19.9 reduce-scatter.36
  942.5 21.6 reduce-scatter.40
  966.7 22.0 reduce-scatter.32

commit v2 on v0

v2 whole, which is shorter than its diff:
```python
import functools
from types import SimpleNamespace

import jax
import jax.numpy as jnp
from jax import lax
from jax.experimental import pallas as pl
from jax.experimental.pallas import tpu as pltpu
from jax.sharding import PartitionSpec as P

MESH = pl.DeviceIdType.MESH
F32 = jnp.float32
BF16 = jnp.bfloat16

HA = 14
WA = 14
HB = 10
WB = 10

EPS = 1e-05
LEAF = 1024
NARROW, SPATIAL, WIDENED, SQUEEZE, STRIDED, OUTPUT, SHORTCUT = range(7)
NEAR = (0, 1, 2, 3, 4)
FAR = (0, 2, 3, 4, 1)
BITS = 5
SHARDS = 1 << BITS
G_REDUCE_ONE, G_SPATIAL_ONE, G_EXPAND_ONE, G_REDUCE_TWO, G_SPATIAL_TWO, G_EXPAND_TWO, G_SHORTCUT_TWO = range(7)
GRADS = (
    (32, 256, NEAR),
    (144, 128, FAR),
    (16, 512, NEAR),
    (32, 512, FAR),
    (144, 512, NEAR),
    (16, 2048, FAR),
    (32, 2048, FAR),
)
(
    AT_ONE,
    AT_TWO,
    AT_THREE,
    AT_FOUR,
    AT_FIVE,
    AT_SHORT,
    AT_SIX,
    AT_SEVEN,
    AT_EIGHT,
    AT_NINE,
    AT_TEN,
    AT_ELEVEN,
    AT_TWELVE,
) = range(13)
SUMS = (
    (2, 256),
    (2, 256),
    (2, 1024),
    (2, 512),
    (2, 512),
    (2, 2048),
    (2, 2048),
    (3, 2048),
    (2, 512),
    (2, 512),
    (2, 1024),
    (2, 256),
    (2, 256),
)


def mm(left, right):
    return lax.dot_general(left, right, (((1,), (0,)), ((), ())), preferred_element_type=F32)


def mm_nt(left, right):
    return lax.dot_general(left, right, (((1,), (1,)), ((), ())), preferred_element_type=F32)


def mm_tn(left, right):
    return lax.dot_general(left, right, (((0,), (0,)), ((), ())), preferred_element_type=F32)


def sigmoid(value):
    return 0.5 + 0.5 * jnp.tanh(0.5 * value)


def slope_of(value):
    sigma = sigmoid(value)
    return sigma * (1.0 + value * (1.0 - sigma))


def flat(block):
    return block.reshape(-1, block.shape[-1])


def col_sum(value):
    return jnp.sum(value, axis=0, keepdims=True)


def wide(mask, lanes):
    return jnp.concatenate([mask] * (lanes // 128), axis=1)


def loop(count, body, init=None):
    if init is None:

        def plain(step, carry):
            body(step)
            return carry

        return lax.fori_loop(0, count, plain, 0)
    return lax.fori_loop(0, count, body, init)


def bit_of(number, bit):
    return lax.rem(number // (1 << bit), 2)


class Kernel:
    def __init__(self, sizes, refs):
        self.d_size, self.r_size, self.live_a, self.live_b = sizes
        self.total = self.d_size * self.r_size
        self.__dict__.update(refs)
        self.d = lax.axis_index("dp")
        self.r = lax.axis_index("rows")
        self.me = self.d * self.r_size + self.r
        self.low = (self.total // SHARDS).bit_length() - 1
        self.shard = self.me // (1 << self.low)
        self.r_bits = self.r_size.bit_length() - 1


    def device(self, number):
        return (number // self.r_size, lax.rem(number, self.r_size))

    def greet(self):
        barrier = pltpu.get_barrier_semaphore()

        def one(step):
            pl.semaphore_signal(
                barrier,
                inc=1,
                device_id=self.device(lax.rem(self.me + step + 1, self.total)),
                device_id_type=MESH,
            )

        loop(self.total - 1, one)

    def greeted(self):
        pl.semaphore_wait(pltpu.get_barrier_semaphore(), self.total - 1)

    def direct(self, name):
        return self.sums[name].direct

    def sum_start(self, name, vectors):
        s = self.sums[name]
        for i, vector in enumerate(vectors):
            s.pay[i : i + 1, :] = vector
        if s.direct:

            def send(step):
                pltpu.make_async_remote_copy(
                    s.pay,
                    s.near.at[self.me],
                    s.sems.at[0],
                    s.sems.at[1],
                    device_id=self.device(lax.rem(self.me + step + 1, self.total)),
                    device_id_type=MESH,
                ).start()

            loop(self.total - 1, send)
            s.near[self.me] = s.pay[...]
        else:
            for step in range(1, self.r_size):
                pltpu.make_async_remote_copy(
                    s.pay,
                    s.near.at[self.r],
                    s.sems.at[0],
                    s.sems.at[1],
                    device_id=(self.d, lax.rem(self.r + step, self.r_size)),
                    device_id_type=MESH,
                ).start()
            s.near[self.r] = s.pay[...]

    def sum_turn(self, name):
        s = self.sums[name]
        if s.direct:
            return
        several = s.near.at[0 : self.r_size - 1]
        pltpu.make_async_copy(several, several, s.sems.at[1]).wait()
        s.mid[...] = jnp.sum(s.near[...], axis=0)

        def send(step):
            pltpu.make_async_remote_copy(
                s.mid,
                s.far.at[self.d],
                s.sems.at[2],
                s.sems.at[3],
                device_id=(lax.rem(self.d + step + 1, self.d_size), self.r),
                device_id_type=MESH,
            ).start()

        loop(self.d_size - 1, send)
        s.far[self.d] = s.mid[...]

    def sum_finish(self, name):
        s = self.sums[name]
        if s.direct:
            many = s.near.at[0 : self.total - 1]
            pltpu.make_async_copy(many, many, s.sems.at[1]).wait()
            return jnp.sum(s.near[...], axis=0)
        many = s.far.at[0 : self.d_size - 1]
        pltpu.make_async_copy(many, many, s.sems.at[3]).wait()
        return jnp.sum(s.far[...], axis=0)

    def sums_sent(self):
        for s in self.sums:
            if s.direct:
                many = s.near.at[0 : self.total - 1]
                pltpu.make_async_copy(many, many, s.sems.at[0]).wait()
            else:
                several = s.near.at[0 : self.r_size - 1]
                pltpu.make_async_copy(several, several, s.sems.at[0]).wait()
                many = s.far.at[0 : self.d_size - 1]
                pltpu.make_async_copy(many, many, s.sems.at[2]).wait()


    def norm_ready(self, norm, totals, count):
        coef = self.coef[norm]
        mean = totals[0:1] / count
        scale = lax.rsqrt(totals[1:2] / count - mean * mean + EPS)
        factor = scale * self.gain[norm][...]
        coef[0:1, :] = factor
        coef[1:2, :] = self.bias[norm][...] - mean * factor
        coef[2:3, :] = mean
        coef[3:4, :] = scale

    def norm_back_ready(self, norm, first, second, count):
        coef = self.coef[norm]
        factor, mean, scale = coef[0:1, :], coef[2:3, :], coef[3:4, :]
        second = second * scale
        self.grad_gain[norm][...] = second
        self.grad_bias[norm][...] = first
        slant = factor * scale * (second / count)
        coef[4:5, :] = slant
        coef[5:6, :] = factor * (first / count) - mean * slant

    def act(self, norm, value, lanes=slice(None)):
        coef = self.coef[norm]
        return value * coef[0:1, lanes] + coef[1:2, lanes]

    def off_mean(self, norm, value, lanes=slice(None)):
        return value - self.coef[norm][2:3, lanes]

    def back(self, norm, slope, value, mask, lanes=slice(None)):
        coef = self.coef[norm]
        grad = slope * coef[0:1, lanes] - value * coef[4:5, lanes] - coef[5:6, lanes]
        return (grad * mask).astype(BF16)


    def to_strip(self, step, src, dst, slot):
        return pltpu.make_async_remote_copy(
            src,
            dst,
            self.halo_send.at[slot],
            self.halo_recv.at[slot],
            device_id=(self.d, self.r + step),
            device_id_type=MESH,
        )


    def place(self, name, shard):
        order = GRADS[name][2]
        if isinstance(shard, int):
            return sum(((shard >> b) & 1) << (BITS - 1 - k) for k, b in enumerate(order))
        where = 0
        for k, b in enumerate(order):
            where = where + bit_of(shard, b) * (1 << (BITS - 1 - k))
        return where

    def halving(self, name, stage):
        order = GRADS[name][2]
        start = 0
        for k in range(stage):
            start = start + bit_of(self.shard, order[k]) * (1 << (BITS - 1 - k))
        half = 1 << (BITS - 1 - stage)
        mine = bit_of(self.shard, order[stage])
        offset = SHARDS - 2 * half
        bit = order[stage] + self.low
        if bit < self.r_bits:
            partner = (self.d, self.r + (1 - 2 * mine) * (1 << bit))
        else:
            partner = (self.d + (1 - 2 * mine) * (1 << (bit - self.r_bits)), self.r)
        return start + mine * half, start + (1 - mine) * half, half, offset, partner

    def grad_copy(self, name, stage):
        rows = GRADS[name][0]
        _, away, half, offset, partner = self.halving(name, stage)
        index = name * BITS + stage
        return pltpu.make_async_remote_copy(
            self.grads[name].at[pl.ds(pl.multiple_of(away * rows, 16), half * rows)],
            self.recv[name].at[pl.ds(offset * rows, half * rows)],
            self.grad_send.at[index],
            self.grad_recv.at[index],
            device_id=partner,
            device_id_type=MESH,
        )

    def grad_start(self, name):
        self.grad_copy(name, 0).start()

    def grad_step(self, name, stage):
        rows, lanes, _ = GRADS[name]
        keep, _, half, offset, _ = self.halving(name, stage)
        self.grad_copy(name, stage).wait_recv()
        own, came = self.grads[name], self.recv[name]
        if stage < BITS - 1:
            height = 16
            while height * lanes < 32768 and (half * rows) % (2 * height) == 0:
                height *= 2

            def add(step):
                here = pl.ds(pl.multiple_of(keep * rows + step * height, 16), height)
                there = pl.ds(pl.multiple_of(offset * rows + step * height, 16), height)
                own[here, :] = (own[here, :].astype(F32) + came[there, :].astype(F32)).astype(BF16)

            loop(half * rows // height, add)
            self.grad_copy(name, stage + 1).start()
            return
        here = pl.ds(pl.multiple_of(keep * rows, 16), rows)
        there = pl.ds(offset * rows, rows)
        out = self.grad_out[name]
        total = own[here, :].astype(F32) + came[there, :].astype(F32)
        if name == G_SPATIAL_ONE:
            for tap in range(9):
                out[tap, :, 0:128] = total[tap * 16 : tap * 16 + 8]
                out[tap, :, 128:256] = total[tap * 16 + 8 : tap * 16 + 16]
        elif name == G_EXPAND_ONE:
            out[:, 0:512] = total[0:8]
            out[:, 512:1024] = total[8:16]
        else:
            out[...] = total

    def grads_sent(self):
        for name in range(len(GRADS)):
            for stage in range(BITS):
                self.grad_copy(name, stage).wait_send()

    def grad_store(self, name, block, value, lanes=slice(None), row=0):
        rows, _, _ = GRADS[name]
        per = 16 if name == G_SPATIAL_TWO else rows
        count = 256 // per
        base = self.place(name, block * count) * rows + row
        for s in range(count):
            where = base + self.place(name, s) * rows
            if not isinstance(where, int):
                where = pl.multiple_of(where, 16)
            self.grads[name][pl.ds(where, per), lanes] = value[s * per : (s + 1) * per].astype(BF16)


    def run(self):
        self.greet()
        pairs = dict(
            xa=(self.xa_in, self.xa),
            xb=(self.xb_in, self.xb),
            w1=(self.w1_in, self.w1),
            ca=(self.ca_in, self.ca),
            cb=(self.cb_in, self.cb),
            w2=(self.w2_in, self.w2),
            w3=(self.w3_in, self.w3),
            w4=(self.w4_in, self.w4),
            ws=(self.ws_in, self.ws),
            w5=(self.w5_in, self.w5),
            w6=(self.w6_in, self.w6),
        )
        loads = SimpleNamespace()
        for i, name in enumerate(pairs):
            copy = pltpu.make_async_copy(*pairs[name], self.load_sem.at[i])
            copy.start()
            setattr(loads, name, copy)

        x, z1, z2, z3, z4, z5 = self.x, self.z1, self.z2, self.z3, self.z4, self.z5
        h1, h2, feed, h4, h5 = self.h1, self.h2, self.feed, self.h4, self.h5
        big, mask = self.big, self.mask
        rows, cols, views, _ = x.shape
        half = cols // 2
        natural = [2 * (k % half) + k // half for k in range(cols)]
        zeros = functools.partial(jnp.zeros, dtype=BF16)

        live_a = self.live[0, self.d]
        live_b = self.live[1, self.d]
        all_a = self.live[0, 0]
        all_b = self.live[1, 0]
        for i in range(1, self.d_size):
            all_a = all_a + self.live[0, i]
            all_b = all_b + self.live[1, i]
        line = jnp.zeros((1, 128), jnp.int32)
        line_a = (line + all_a).astype(F32)
        line_b = (line + all_b).astype(F32)
        full_one = HA * WA * line_a + HB * WB * line_b
        half_one = ((HA + 1) // 2) * ((WA + 1) // 2) * line_a + ((HB + 1) // 2) * (
            (WB + 1) // 2
        ) * line_b
        self.full_count[...] = full_one
        self.half_count[...] = half_one

        def full(lanes):
            return wide(self.full_count[...], lanes)

        def part(lanes):
            return wide(self.half_count[...], lanes)

        def make_mask(row):
            place = lax.broadcasted_iota(jnp.int32, (cols, views, 128), 0)
            column = jnp.where(place < half, 2 * place, 2 * (place - half) + 1)
            view = lax.broadcasted_iota(jnp.int32, (cols, views, 128), 1)
            where = self.r * rows + row
            tall_a = jnp.where(where < HA, live_a, 0)
            tall_b = jnp.where(where < HB, live_b, 0)
            in_a = (view < self.live_a) & (view < tall_a)
            in_b = (view >= self.live_a) & (view - self.live_a < tall_b) & (column < WB)
            mask[row] = jnp.where(in_a | in_b, 1.0, 0.0).astype(F32)

        loop(rows, make_mask)

        for ref in (h1, self.dz2):
            lanes = ref.shape[-1]
            ref[0] = zeros((cols + 2, views, lanes))
            ref[rows + 1] = zeros((cols + 2, views, lanes))
            for row in range(1, rows + 1):
                ref[row, 0] = zeros((views, lanes))
                ref[row, cols + 1] = zeros((views, lanes))
        h4[0] = zeros(h4.shape[1:])
        for row in range(1, rows + 1):
            h4[row, half] = zeros((views, h4.shape[-1]))
        self.dz5[rows // 2] = zeros(self.dz5.shape[1:])
        for row in range(rows // 2):
            self.dz5[row, half] = zeros((views, self.dz5.shape[-1]))

        def row_mask(row, lanes):
            return wide(flat(mask[row]), lanes)

        none = jnp.zeros((1, 256), F32)

        loads.xa.wait()
        loads.xb.wait()

        def gather_row(row):
            for k in range(cols):
                c = natural[k]
                near = self.xa[row, c].astype(F32)
                if c < self.xb.shape[1]:
                    rest = self.xb[row, c].astype(F32)
                else:
                    rest = jnp.zeros((self.live_b, near.shape[-1]), F32)
                value = jnp.concatenate([near, rest], axis=0)
                x[row, k] = (value * wide(mask[row, k], value.shape[-1])).astype(BF16)

        loop(rows, gather_row)
        loads.w1.wait()

        def reduce_row(row, carry):
            total, square = carry
            value = mm(flat(x[row]), self.w1[...])
            z1[row] = value.reshape(cols, views, -1)
            return (total + col_sum(value), square + col_sum(value * value))

        sums = loop(rows, reduce_row, (none, none))
        self.greeted()
        self.sum_start(AT_ONE, sums)
        self.sum_turn(AT_ONE)
        loads.ca.wait()
        loads.cb.wait()
        for o in range(rows // 2):
            for p in range(half):
                for h in range(2):
                    lanes = slice(h * LEAF, h * LEAF + LEAF)
                    near = self.ca[o, p, :, lanes].astype(F32)
                    if p < self.cb.shape[1]:
                        rest = self.cb[o, p, :, lanes].astype(F32)
                    else:
                        rest = jnp.zeros((self.live_b, LEAF), F32)
                    self.cot[h, o * half + p] = jnp.concatenate([near, rest], axis=0).astype(BF16)
        self.norm_ready(NARROW, self.sum_finish(AT_ONE), full(256))

        def hidden_one(row):
            value = self.act(NARROW, flat(z1[row]))
            value = (value * sigmoid(value) * row_mask(row, 256)).astype(BF16)
            value = value.reshape(cols, views, -1)
            for k in range(cols):
                h1[row + 1, natural[k] + 1] = value[k]

        first, last = self.r == 0, self.r == self.r_size - 1
        hidden_one(0)
        hidden_one(rows - 1)
        up = self.to_strip(-1, h1.at[1], h1.at[rows + 1], 0)
        down = self.to_strip(1, h1.at[rows], h1.at[0], 1)

        @pl.when(jnp.logical_not(first))
        def _():
            up.start()

        @pl.when(jnp.logical_not(last))
        def _():
            down.start()

        loop(rows - 2, lambda i: hidden_one(i + 1))
        loads.w2.wait()

        def conv_row(row, carry):
            total, square = carry
            value = 0.0
            for i in range(3):
                for j in range(3):
                    tap = (i * 3 + j) * 256
                    value = value + mm(flat(h1[row + i, j : j + cols]), self.w2[tap : tap + 256, :])
            value = value.reshape(cols, views, -1)
            ordered = jnp.concatenate([value[c] for c in natural], axis=0)
            z2[row] = ordered.reshape(cols, views, -1)
            kept = ordered * row_mask(row, 256)
            return (total + col_sum(kept), square + col_sum(kept * ordered))

        sums = loop(rows - 2, lambda i, carry: conv_row(i + 1, carry), (none, none))

        @pl.when(jnp.logical_not(last))
        def _():
            self.to_strip(1, h1.at[rows], h1.at[rows + 1], 0).wait_recv()

        @pl.when(jnp.logical_not(first))
        def _():
            self.to_strip(-1, h1.at[1], h1.at[0], 1).wait_recv()

        sums = conv_row(rows - 1, conv_row(0, sums))
        self.sum_start(AT_TWO, sums)
        self.sum_turn(AT_TWO)
        loads.w3.wait()
        self.norm_ready(SPATIAL, self.sum_finish(AT_TWO), full(256))

        def hidden_two(row):
            value = self.act(SPATIAL, flat(z2[row]))
            value = (value * sigmoid(value) * row_mask(row, 256)).astype(BF16)
            h2[row] = value.reshape(cols, views, -1)

        loop(rows, hidden_two)

        def expand_row(row, carry):
            given = flat(h2[row])
            done = []
            for n in range(2):
                lanes = slice(n * 512, n * 512 + 512)
                value = mm(given, self.w3[:, lanes])
                z3[row, :, :, lanes] = value.reshape(cols, views, -1)
                done.append((carry[n][0] + col_sum(value), carry[n][1] + col_sum(value * value)))
            return tuple(done)

        nothing = jnp.zeros((1, 512), F32)
        sums = loop(rows, expand_row, ((nothing, nothing), (nothing, nothing)))
        sums = [jnp.concatenate([sums[0][i], sums[1][i]], axis=1) for i in range(2)]
        self.sum_start(AT_THREE, sums)
        self.sum_turn(AT_THREE)
        loads.w4.wait()
        loads.ws.wait()
        self.norm_ready(WIDENED, self.sum_finish(AT_THREE), full(1024))

        def feed_step(step):
            row, pair = step // half, lax.rem(step, half)
            here = pl.ds(pair * 2, 2)
            value = self.act(WIDENED, flat(z3[row, here])) + flat(x[row, here]).astype(F32)
            value = value * sigmoid(value) * wide(flat(mask[row, here]), 1024)
            feed[row, here] = value.astype(BF16).reshape(2, views, -1)

        loop(rows * half, feed_step)

        def squeeze_row(row, carry):
            total, square = carry
            value = mm(flat(feed[row]), self.w4[...])
            z4[row] = value.reshape(cols, views, -1)
            return (total + col_sum(value), square + col_sum(value * value))

        sums = loop(rows, squeeze_row, (nothing, nothing))
        self.sum_start(AT_FOUR, sums)
        self.sum_turn(AT_FOUR)

        def even(ref):
            return jnp.concatenate([flat(ref[2 * o, 0:half]) for o in range(rows // 2)], axis=0)

        for h in range(2):
            sums = []
            for n in range(2):
                lanes = slice(h * LEAF + n * 512, h * LEAF + n * 512 + 512)
                value = mm(even(feed), self.ws[:, lanes])
                big[2 + h, :, :, n * 512 : n * 512 + 512] = value.reshape(cols, views, -1)
                sums.append((col_sum(value), col_sum(value * value)))
            for i in range(2):
                self.short_sum[i : i + 1, h * LEAF : h * LEAF + LEAF] = jnp.concatenate(
                    [sums[0][i], sums[1][i]], axis=1
                )
        self.sum_start(AT_SHORT, [self.short_sum[0:1, :], self.short_sum[1:2, :]])
        self.norm_ready(SQUEEZE, self.sum_finish(AT_FOUR), full(512))

        def hidden_four(row):
            for p in range(2):
                value = self.act(SQUEEZE, flat(z4[row, p * half : p * half + half]))
                value = value * sigmoid(value) * wide(flat(mask[row, p * half : p * half + half]), 512)
                start = p * (half + 1)
                h4[row + 1, start : start + half] = value.astype(BF16).reshape(half, views, -1)

        hidden_four(rows - 1)
        below = self.to_strip(1, h4.at[rows], h4.at[0], 2)

        @pl.when(jnp.logical_not(last))
        def _():
            below.start()

        loop(rows - 1, hidden_four)
        loads.w5.wait()
        starts = (half, 0, half + 1)

        def taken(i, j):
            return jnp.concatenate(
                [flat(h4[2 * o + i, starts[j] : starts[j] + half]) for o in range(rows // 2)], axis=0
            )

        value = 0.0
        for i in (1, 2, 0):
            if i == 0:

                @pl.when(jnp.logical_not(first))
                def _():
                    self.to_strip(-1, h4.at[rows], h4.at[0], 2).wait_recv()

            for j in range(3):
                tap = (i * 3 + j) * 512
                value = value + mm(taken(i, j), self.w5[tap : tap + 512, :])
        z5[...] = value
        half_mask = jnp.concatenate(
            [flat(mask[2 * o, 0:half]) for o in range(rows // 2)], axis=0
        )
        self.half_mask[...] = half_mask
        kept = value * wide(half_mask, 512)
        self.sum_start(AT_FIVE, (col_sum(kept), col_sum(kept * value)))
        self.sum_turn(AT_FIVE)
        self.sum_turn(AT_SHORT)
        loads.w6.wait()
        self.norm_ready(STRIDED, self.sum_finish(AT_FIVE), part(512))
        value = self.act(STRIDED, z5[...])
        h5[...] = (value * sigmoid(value) * wide(self.half_mask[...], 512)).astype(BF16)

        for h in range(2):
            sums = []
            for n in range(2):
                lanes = slice(h * LEAF + n * 512, h * LEAF + n * 512 + 512)
                value = mm(h5[...], self.w6[:, lanes])
                big[h, :, :, n * 512 : n * 512 + 512] = value.reshape(cols, views, -1)
                sums.append((col_sum(value), col_sum(value * value)))
            for i in range(2):
                self.main_sum[i : i + 1, h * LEAF : h * LEAF + LEAF] = jnp.concatenate(
                    [sums[0][i], sums[1][i]], axis=1
                )
        self.sum_start(AT_SIX, [self.main_sum[0:1, :], self.main_sum[1:2, :]])
        self.norm_ready(SHORTCUT, self.sum_finish(AT_SHORT), part(2048))
        self.sum_turn(AT_SIX)
        self.norm_ready(OUTPUT, self.sum_finish(AT_SIX), part(2048))

        top, cot = self.top, self.cot
        zero = jnp.zeros((1, LEAF), F32)
        for h in range(2):
            lanes = slice(h * LEAF, h * LEAF + LEAF)

            def out_step(pair, carry):
                here = pl.ds(pair * 2, 2)
                main, side = flat(big[h, here]), flat(big[2 + h, here])
                value = self.act(OUTPUT, main, lanes) + self.act(SHORTCUT, side, lanes)
                there = wide(self.half_mask[pl.ds(pl.multiple_of(pair * 2 * views, 8), 2 * views), :], LEAF)
                sigma = sigmoid(value)
                given = flat(cot[h, here]).astype(F32)
                slope = given * there * (sigma * (1.0 + value * (1.0 - sigma)))
                cot[h, here] = (value * sigma * there).astype(BF16).reshape(2, views, -1)
                top[h, here] = slope.reshape(2, views, -1)
                return (
                    carry[0] + col_sum(slope),
                    carry[1] + col_sum(slope * self.off_mean(OUTPUT, main, lanes)),
                    carry[2] + col_sum(slope * self.off_mean(SHORTCUT, side, lanes)),
                )

            sums = loop(half, out_step, (zero, zero, zero))
            for i in range(3):
                self.top_sum[i : i + 1, lanes] = sums[i]
        self.sum_start(AT_SEVEN, [self.top_sum[i : i + 1, :] for i in range(3)])
        for o in range(rows // 2):
            for p in range(half):
                for h in range(2):
                    lanes = slice(h * LEAF, h * LEAF + LEAF)
                    done = cot[h, o * half + p].astype(F32)
                    self.ca[o, p, :, lanes] = done[0 : self.live_a].astype(BF16)
                    if p < self.cb.shape[1]:
                        self.cb[o, p, :, lanes] = done[self.live_a :].astype(BF16)
        stores = [
            pltpu.make_async_copy(self.ca, self.out_a_to, self.store_sem.at[0]),
            pltpu.make_async_copy(self.cb, self.out_b_to, self.store_sem.at[1]),
        ]
        for copy in stores:
            copy.start()
        self.sum_turn(AT_SEVEN)
        totals = self.sum_finish(AT_SEVEN)
        self.norm_back_ready(OUTPUT, totals[0:1], totals[1:2], part(2048))
        self.norm_back_ready(SHORTCUT, totals[0:1], totals[2:3], part(2048))

        dz6, dzs = self.dz6, self.dzs
        for h in range(2):
            lanes = slice(h * LEAF, h * LEAF + LEAF)

            def top_step(pair):
                here = pl.ds(pair * 2, 2)
                there = pl.ds(pl.multiple_of(pair * 2 * views, 16), 2 * views)
                live = wide(self.half_mask[there, :], LEAF)
                slope = flat(top[h, here])
                dz6[there, lanes] = self.back(OUTPUT, slope, flat(big[h, here]), live, lanes)
                dzs[there, lanes] = self.back(SHORTCUT, slope, flat(big[2 + h, here]), live, lanes)

            loop(half, top_step)

        value = mm_nt(dz6[...], self.w6[...]) * slope_of(self.act(STRIDED, z5[...]))
        self.slope5[...] = value
        self.sum_start(AT_EIGHT, (col_sum(value), col_sum(value * self.off_mean(STRIDED, z5[...]))))

        def clear(row):
            big[row] = jnp.zeros(big.shape[1:], F32)

        def shortcut_back(n):
            lanes = pl.ds(pl.multiple_of(n * 256, 256), 256)
            value = mm_nt(dzs[...], self.ws[lanes, :]).reshape(rows // 2, half, views, -1)
            for o in range(rows // 2):
                big[2 * o, 0:half, :, lanes] = value[o]

        def grad_expand_two(step):
            m, n = step // 4, lax.rem(step, 4)
            left = h5[:, pl.ds(pl.multiple_of(m * 256, 256), 256)]
            lanes = pl.ds(pl.multiple_of(n * 512, 512), 512)
            self.grad_store(G_EXPAND_TWO, m, mm_tn(left, dz6[:, lanes]), lanes)

        def grad_shortcut_two(step):
            m, n = step // 4, lax.rem(step, 4)
            here = pl.ds(pl.multiple_of(m * 256, 256), 256)
            left = jnp.concatenate(
                [flat(feed[2 * o, 0:half, :, here]) for o in range(rows // 2)], axis=0
            )
            lanes = pl.ds(pl.multiple_of(n * 512, 512), 512)
            self.grad_store(G_SHORTCUT_TWO, m, mm_tn(left, dzs[:, lanes]), lanes)

        loop(8, grad_expand_two)
        self.grad_start(G_EXPAND_TWO)
        self.sum_turn(AT_EIGHT)
        loop(rows, clear)
        loop(4, shortcut_back)
        totals = self.sum_finish(AT_EIGHT)
        self.norm_back_ready(STRIDED, totals[0:1], totals[1:2], part(512))
        dz5 = self.dz5
        value = self.back(STRIDED, self.slope5[...], z5[...], wide(self.half_mask[...], 512))
        for o in range(rows // 2):
            dz5[o, 0:half] = value[o * half * views : (o + 1) * half * views].reshape(half, views, -1)
        above = self.to_strip(-1, dz5.at[0], dz5.at[rows // 2], 3)

        @pl.when(jnp.logical_not(first))
        def _():
            above.start()

        loop(16, grad_shortcut_two)
        self.grad_start(G_SHORTCUT_TWO)
        self.grad_step(G_EXPAND_TWO, 0)

        dh4 = self.dh4
        for i in (1, 2, 0):
            if i == 0:

                @pl.when(jnp.logical_not(last))
                def _():
                    self.to_strip(1, dz5.at[0], dz5.at[rows // 2], 3).wait_recv()

            lead = 1 if i == 0 else 0
            for j in (1, 2, 0):
                tap = (i * 3 + j) * 512
                start = 1 if j == 0 else 0
                given = jnp.concatenate(
                    [flat(dz5[o + lead, start : start + half]) for o in range(rows // 2)], axis=0
                )
                value = mm_nt(given, self.w5[tap : tap + 512, :]).reshape(rows // 2, half, views, -1)
                spot = slice(0, half) if j == 1 else slice(half, 2 * half)
                for o in range(rows // 2):
                    target = 2 * o if i == 1 else 2 * o + 1
                    if j == 0 or i == 0:
                        dh4[target, spot] = dh4[target, spot] + value[o]
                    else:
                        dh4[target, spot] = value[o]

        def slope_four(step, carry):
            row, p = step // 2, lax.rem(step, 2)
            here = pl.ds(p * half, half)
            before = flat(z4[row, here])
            value = flat(dh4[row, here]) * slope_of(self.act(SQUEEZE, before))
            dh4[row, here] = value.reshape(half, views, -1)
            return (
                carry[0] + col_sum(value),
                carry[1] + col_sum(value * self.off_mean(SQUEEZE, before)),
            )

        sums = loop(rows * 2, slope_four, (nothing, nothing))
        self.sum_start(AT_NINE, sums)
        self.sum_turn(AT_NINE)
        self.grad_step(G_SHORTCUT_TWO, 0)
        self.grad_step(G_EXPAND_TWO, 1)
        for j in range(3):

            def grad_spatial_two(step):
                i, m = step // 2, lax.rem(step, 2)
                here = pl.ds(pl.multiple_of(m * 256, 256), 256)
                left = jnp.concatenate(
                    [
                        flat(h4[2 * o + i, starts[j] : starts[j] + half, :, here])
                        for o in range(rows // 2)
                    ],
                    axis=0,
                )
                right = jnp.concatenate([flat(dz5[o, 0:half]) for o in range(rows // 2)], axis=0)
                self.grad_store(G_SPATIAL_TWO, m, mm_tn(left, right), row=(i * 3 + j) * 16)

            loop(6, grad_spatial_two)
        self.grad_start(G_SPATIAL_TWO)
        totals = self.sum_finish(AT_NINE)
        self.norm_back_ready(SQUEEZE, totals[0:1], totals[1:2], full(512))
        dz4 = self.dz4

        def back_four(step):
            row, p = step // 2, lax.rem(step, 2)
            here = pl.ds(p * half, half)
            value = self.back(
                SQUEEZE, flat(dh4[row, here]), flat(z4[row, here]), wide(flat(mask[row, here]), 512)
            )
            dz4[row, here] = value.reshape(half, views, -1)

        loop(rows * 2, back_four)

        def slope_three(row, carry):
            done = []
            for n in range(2):
                lanes = slice(n * 512, n * 512 + 512)
                before = flat(z3[row, :, :, lanes])
                grad = mm_nt(flat(dz4[row]), self.w4[lanes, :]) + flat(big[row, :, :, lanes])
                point = self.act(WIDENED, before, lanes) + flat(x[row, :, :, lanes]).astype(F32)
                value = grad * slope_of(point)
                big[row, :, :, lanes] = value.reshape(cols, views, -1)
                done.append(
                    (
                        carry[n][0] + col_sum(value),
                        carry[n][1] + col_sum(value * self.off_mean(WIDENED, before, lanes)),
                    )
                )
            return tuple(done)

        sums = loop(rows, slope_three, ((nothing, nothing), (nothing, nothing)))
        sums = [jnp.concatenate([sums[0][i], sums[1][i]], axis=1) for i in range(2)]
        self.sum_start(AT_TEN, sums)
        self.grad_step(G_SHORTCUT_TWO, 1)
        self.sum_turn(AT_TEN)
        self.grad_step(G_SPATIAL_TWO, 0)
        self.grad_step(G_EXPAND_TWO, 2)

        def grad_reduce_two(m):
            here = pl.ds(pl.multiple_of(m * 256, 256), 256)
            left = feed[:, :, :, here].reshape(-1, 256)
            self.grad_store(G_REDUCE_TWO, m, mm_tn(left, dz4[...].reshape(-1, 512)))

        loop(4, grad_reduce_two)
        self.grad_start(G_REDUCE_TWO)
        totals = self.sum_finish(AT_TEN)
        self.norm_back_ready(WIDENED, totals[0:1], totals[1:2], full(1024))
        dz3 = feed

        def back_three(step):
            row, pair = step // half, lax.rem(step, half)
            here = pl.ds(pair * 2, 2)
            live = wide(flat(mask[row, here]), 1024)
            value = self.back(WIDENED, flat(big[row, here]), flat(z3[row, here]), live)
            dz3[row, here] = value.reshape(2, views, -1)

        loop(rows * half, back_three)


        def slope_spatial(row, carry):
            before = flat(z2[row])
            value = mm_nt(flat(dz3[row]), self.w3[...]) * slope_of(self.act(SPATIAL, before))
            dh4[row, :, :, 0:256] = value.reshape(cols, views, -1)
            return (
                carry[0] + col_sum(value),
                carry[1] + col_sum(value * self.off_mean(SPATIAL, before)),
            )

        sums = loop(rows, slope_spatial, (none, none))
        self.sum_start(AT_ELEVEN, sums)
        self.sum_turn(AT_ELEVEN)

        left = h2[...].reshape(-1, 256)
        g_low = mm_tn(left, dz3[:, :, :, 0:512].reshape(-1, 512))
        g_high = mm_tn(left, dz3[:, :, :, 512:1024].reshape(-1, 512))
        for s in range(SHARDS):
            at = self.place(G_EXPAND_ONE, s) * 16
            piece = jnp.concatenate([g_low[s * 8 : s * 8 + 8], g_high[s * 8 : s * 8 + 8]], axis=0)
            self.grads[G_EXPAND_ONE][at : at + 16, :] = piece.astype(BF16)
        self.grad_start(G_EXPAND_ONE)
        self.grad_step(G_SPATIAL_TWO, 1)
        self.grad_step(G_REDUCE_TWO, 0)
        totals = self.sum_finish(AT_ELEVEN)
        self.norm_back_ready(SPATIAL, totals[0:1], totals[1:2], full(256))
        dz2 = self.dz2

        def back_two(row):
            value = self.back(SPATIAL, flat(dh4[row, :, :, 0:256]), flat(z2[row]), row_mask(row, 256))
            value = value.reshape(cols, views, -1)
            for k in range(cols):
                dz2[row + 1, natural[k] + 1] = value[k]

        back_two(0)
        back_two(rows - 1)
        up = self.to_strip(-1, dz2.at[1], dz2.at[rows + 1], 4)
        down = self.to_strip(1, dz2.at[rows], dz2.at[0], 5)

        @pl.when(jnp.logical_not(first))
        def _():
            up.start()

        @pl.when(jnp.logical_not(last))
        def _():
            down.start()

        loop(rows - 2, lambda i: back_two(i + 1))
        for i in range(3):
            for j in range(3):
                left = h1[i : i + rows, j : j + cols].reshape(-1, 256)
                value = mm_tn(left, dz2[1 : rows + 1, 1 : cols + 1].reshape(-1, 256))
                for s in range(SHARDS):
                    at = self.place(G_SPATIAL_ONE, s) * 144 + (i * 3 + j) * 16
                    piece = value[s * 8 : s * 8 + 8]
                    piece = jnp.concatenate([piece[:, 0:128], piece[:, 128:256]], axis=0)
                    self.grads[G_SPATIAL_ONE][at : at + 16, :] = piece.astype(BF16)
        self.grad_start(G_SPATIAL_ONE)

        @pl.when(jnp.logical_not(last))
        def _():
            self.to_strip(1, dz2.at[rows], dz2.at[rows + 1], 4).wait_recv()

        @pl.when(jnp.logical_not(first))
        def _():
            self.to_strip(-1, dz2.at[1], dz2.at[0], 5).wait_recv()

        def slope_narrow(row, carry):
            value = 0.0
            for i in range(3):
                for j in range(3):
                    tap = (i * 3 + j) * 256
                    given = flat(dz2[row + 2 - i, 2 - j : 2 - j + cols])
                    value = value + mm_nt(given, self.w2[tap : tap + 256, :])
            value = value.reshape(cols, views, -1)
            value = jnp.concatenate([value[c] for c in natural], axis=0)
            before = flat(z1[row])
            value = value * row_mask(row, 256) * slope_of(self.act(NARROW, before))
            dh4[row, :, :, 0:256] = value.reshape(cols, views, -1)
            return (
                carry[0] + col_sum(value),
                carry[1] + col_sum(value * self.off_mean(NARROW, before)),
            )

        sums = loop(rows, slope_narrow, (none, none))
        self.sum_start(AT_TWELVE, sums)
        self.sum_turn(AT_TWELVE)
        self.grad_step(G_EXPAND_ONE, 0)
        self.grad_step(G_SPATIAL_ONE, 0)
        self.grad_step(G_SHORTCUT_TWO, 2)
        self.grad_step(G_SPATIAL_TWO, 2)
        self.grad_step(G_REDUCE_TWO, 1)
        self.grad_step(G_EXPAND_TWO, 3)
        totals = self.sum_finish(AT_TWELVE)
        self.norm_back_ready(NARROW, totals[0:1], totals[1:2], full(256))
        dz1 = h2

        def back_one(row):
            value = self.back(NARROW, flat(dh4[row, :, :, 0:256]), flat(z1[row]), row_mask(row, 256))
            dz1[row] = value.reshape(cols, views, -1)

        loop(rows, back_one)

        def grad_reduce_one(m):
            here = pl.ds(pl.multiple_of(m * 256, 256), 256)
            left = x[:, :, :, here].reshape(-1, 256)
            self.grad_store(G_REDUCE_ONE, m, mm_tn(left, dz1[...].reshape(-1, 256)))

        loop(4, grad_reduce_one)
        self.grad_start(G_REDUCE_ONE)

        def input_row(row):
            for n in range(2):
                lanes = slice(n * 512, n * 512 + 512)
                value = mm_nt(flat(dz1[row]), self.w1[lanes, :]) + flat(big[row, :, :, lanes])
                value = value.reshape(cols, views, -1)
                for k in range(cols):
                    self.xa[row, natural[k], :, lanes] = value[k, 0 : self.live_a].astype(BF16)
                    if natural[k] < self.xb.shape[1]:
                        self.xb[row, natural[k], :, lanes] = value[k, self.live_a :].astype(BF16)

        loop(rows, input_row)
        for i, pair in enumerate(((self.xa, self.in_a_to), (self.xb, self.in_b_to))):
            copy = pltpu.make_async_copy(*pair, self.store_sem.at[2 + i])
            copy.start()
            stores.append(copy)
        for name, stage in (
            (G_EXPAND_ONE, 1),
            (G_SPATIAL_ONE, 1),
            (G_REDUCE_ONE, 0),
            (G_SHORTCUT_TWO, 3),
            (G_SPATIAL_TWO, 3),
            (G_REDUCE_TWO, 2),
            (G_EXPAND_TWO, 4),
            (G_EXPAND_ONE, 2),
            (G_SPATIAL_ONE, 2),
            (G_REDUCE_ONE, 1),
            (G_SHORTCUT_TWO, 4),
            (G_SPATIAL_TWO, 4),
            (G_REDUCE_TWO, 3),
            (G_EXPAND_ONE, 3),
            (G_SPATIAL_ONE, 3),
            (G_REDUCE_ONE, 2),
            (G_REDUCE_TWO, 4),
            (G_EXPAND_ONE, 4),
            (G_SPATIAL_ONE, 4),
            (G_REDUCE_ONE, 3),
            (G_REDUCE_ONE, 4),
        ):
            self.grad_step(name, stage)

        for copy in stores:
            copy.wait()
        self.sums_sent()
        self.grads_sent()

        @pl.when(jnp.logical_not(first))
        def _():
            self.to_strip(-1, h1.at[1], h1.at[rows + 1], 0).wait_send()
            self.to_strip(-1, dz5.at[0], dz5.at[rows // 2], 3).wait_send()
            self.to_strip(-1, dz2.at[1], dz2.at[rows + 1], 4).wait_send()

        @pl.when(jnp.logical_not(last))
        def _():
            self.to_strip(1, h1.at[rows], h1.at[0], 1).wait_send()
            self.to_strip(1, h4.at[rows], h4.at[0], 2).wait_send()
            self.to_strip(1, dz2.at[rows], dz2.at[0], 5).wait_send()


def settle(*refs):
    half = len(refs) // 2
    for i in range(half):
        refs[half + i][...] = refs[i][...]


def settled(values):
    inside = pl.BlockSpec(memory_space=pltpu.VMEM)
    return pl.pallas_call(
        settle,
        out_shape=[jax.ShapeDtypeStruct(v.shape, v.dtype) for v in values],
        in_specs=[inside] * len(values),
        out_specs=[inside] * len(values),
    )(*values)


def sum_of(pay, near, mid, far, sems):
    return SimpleNamespace(direct=far is None, pay=pay, near=near, mid=mid, far=far, sems=sems)


def both_blocks(given, live_views, weights, gains, biases):
    d_size, r_size = lax.axis_size("dp"), lax.axis_size("rows")
    total = d_size * r_size
    rows, cols, views_a, c_in = given[0].shape
    views_b = given[1].shape[2]
    views = views_a + views_b
    half = cols // 2
    c_mid, c_mid2, c_out = gains[0].shape[1], gains[3].shape[1], gains[5].shape[1]
    pixels = (rows // 2) * half * views
    vmem, dma = pltpu.VMEM, pltpu.SemaphoreType.DMA
    anywhere = pl.BlockSpec(memory_space=pl.ANY)
    inside = pl.BlockSpec(memory_space=pltpu.VMEM)

    def full(lanes, kind):
        return vmem((rows, cols, views, lanes), kind)

    def like(value):
        return vmem(value.shape, value.dtype)

    sums = []
    for count, lanes in SUMS:
        direct = lanes <= 512 and total <= 32
        sums.append(
            dict(
                pay=vmem((count, lanes), F32),
                near=vmem((total if direct else r_size, count, lanes), F32),
                mid=None if direct else vmem((count, lanes), F32),
                far=None if direct else vmem((d_size, count, lanes), F32),
                sems=dma((4,)),
            )
        )
    w = weights
    scratch = dict(
        xa=like(given[0]),
        xb=like(given[1]),
        ca=like(given[2]),
        cb=like(given[3]),
        x=full(c_in, BF16),
        w1=like(w[0]),
        w2=like(w[1]),
        w3=like(w[2]),
        w4=like(w[3]),
        w5=like(w[4]),
        w6=like(w[5]),
        ws=like(w[6]),
        cot=vmem((2, cols, views, LEAF), BF16),
        mask=full(128, F32),
        half_mask=vmem((pixels, 128), F32),
        full_count=vmem((1, 128), F32),
        half_count=vmem((1, 128), F32),
        z1=full(c_mid, F32),
        z2=full(c_mid, F32),
        z3=full(c_in, F32),
        z4=full(c_mid2, F32),
        z5=vmem((pixels, c_mid2), F32),
        h1=vmem((rows + 2, cols + 2, views, c_mid), BF16),
        h2=full(c_mid, BF16),
        feed=full(c_in, BF16),
        h4=vmem((rows + 1, cols + 1, views, c_mid2), BF16),
        h5=vmem((pixels, c_mid2), BF16),
        big=full(c_in, F32),
        top=vmem((2, cols, views, LEAF), F32),
        short_sum=vmem((2, c_out), F32),
        main_sum=vmem((2, c_out), F32),
        top_sum=vmem((3, c_out), F32),
        dz6=vmem((pixels, c_out), BF16),
        dzs=vmem((pixels, c_out), BF16),
        slope5=vmem((pixels, c_mid2), F32),
        dz5=vmem((rows // 2 + 1, half + 1, views, c_mid2), BF16),
        dh4=full(c_mid2, F32),
        dz4=full(c_mid2, BF16),
        dz2=vmem((rows + 2, cols + 2, views, c_mid), BF16),
        g2=vmem((SHARDS * 144, 128), BF16),
        g3=vmem((SHARDS * 16, 512), BF16),
        load_sem=dma((11,)),
        store_sem=dma((4,)),
        halo_send=dma((6,)),
        halo_recv=dma((6,)),
        grad_send=dma((len(GRADS) * BITS,)),
        grad_recv=dma((len(GRADS) * BITS,)),
        coef=[vmem((8, gain.shape[1]), F32) for gain in gains],
        recv=[vmem(((SHARDS - 1) * height, lanes), BF16) for height, lanes, _ in GRADS],
        sums=sums,
    )
    grad_shapes = ((32, 256), (9, 8, 256), (8, 1024), (32, 512), (144, 512), (16, 2048), (32, 2048))
    ins = dict(
        live=live_views,
        xa_in=given[0],
        xb_in=given[1],
        ca_in=given[2],
        cb_in=given[3],
        w1_in=w[0],
        w2_in=w[1],
        w3_in=w[2],
        w4_in=w[3],
        w5_in=w[4],
        w6_in=w[5],
        ws_in=w[6],
        gain=list(gains),
        bias=list(biases),
    )
    shape = jax.ShapeDtypeStruct
    outs = dict(
        out_a_to=shape(given[2].shape, BF16),
        out_b_to=shape(given[3].shape, BF16),
        in_a_to=shape(given[0].shape, BF16),
        in_b_to=shape(given[1].shape, BF16),
        grad_out=[shape(s, F32) for s in grad_shapes],
        grad_gain=[shape(g.shape, F32) for g in gains],
        grad_bias=[shape(g.shape, F32) for g in gains],
    )
    parts = []
    trees = []
    for group in (ins, outs, scratch):
        leaves, tree = jax.tree.flatten(group, is_leaf=lambda v: not isinstance(v, (dict, list, type(None))))
        parts.append(leaves)
        trees.append(tree)
    in_specs = dict(ins)
    for name in ins:
        in_specs[name] = [inside] * len(gains) if isinstance(ins[name], list) else anywhere
    in_specs.update(live=pl.BlockSpec(memory_space=pltpu.SMEM))
    out_specs = {
        name: [inside] * len(outs[name]) if isinstance(outs[name], list) else anywhere for name in outs
    }
    spec_leaves = [
        jax.tree.flatten(group, is_leaf=lambda v: isinstance(v, pl.BlockSpec))[0]
        for group in (in_specs, out_specs)
    ]

    def body(*refs):
        fields = {}
        start = 0
        for leaves, tree in zip(parts, trees):
            fields.update(jax.tree.unflatten(tree, refs[start : start + len(leaves)]))
            start += len(leaves)
        g = SimpleNamespace(**fields)
        fields.update(
            grads=[g.w2, g.g2, g.g3, g.w4, g.w5, g.w6, g.ws],
            sums=[sum_of(**s) for s in g.sums],
        )
        Kernel((d_size, r_size, views_a, views_b), fields).run()

    results = pl.pallas_call(
        body,
        out_shape=parts[1],
        in_specs=spec_leaves[0],
        out_specs=spec_leaves[1],
        scratch_shapes=parts[2],
        compiler_params=pltpu.CompilerParams(
            collective_id=0, has_side_effects=True, vmem_limit_bytes=64 * 2**20 - 65536 * 4
        ),
        cost_estimate=pl.CostEstimate(flops=16 * 10**9, bytes_accessed=30 * 10**6, transcendentals=4 * 10**6),
    )(*parts[0])
    done = SimpleNamespace(**jax.tree.unflatten(trees[1], results))
    plain = settled([done.out_a_to, done.in_a_to, *done.grad_out, *done.grad_gain, *done.grad_bias])
    return plain[0], done.out_b_to, plain[1], done.in_b_to, list(plain[2:9]), plain[9:]


def on_device(input_a, input_b, live_views, *rest):
    weights, params, cotangents = rest[:7], rest[7:21], rest[21:]
    gains = [value.reshape(1, -1) for value in params[0::2]]
    biases = [value.reshape(1, -1) for value in params[1::2]]
    reduce_one, spatial_one, expand_one, reduce_two, spatial_two, expand_two, shortcut_two = weights
    weights = (
        reduce_one,
        spatial_one.transpose(1, 2, 0, 3).reshape(-1, spatial_one.shape[-1]),
        expand_one,
        reduce_two,
        spatial_two.transpose(1, 2, 0, 3).reshape(-1, spatial_two.shape[-1]),
        expand_two,
        shortcut_two,
    )
    given = [value.transpose(0, 2, 1, 3) for value in (input_a, input_b, *cotangents)]
    *moved, grads, norms = both_blocks(given, live_views.T, weights, gains, biases)
    maps = [value.transpose(0, 2, 1, 3) for value in moved]
    grads[1] = grads[1].reshape(3, 3, -1, grads[1].shape[-1]).transpose(2, 0, 1, 3)
    grads[4] = grads[4].reshape(3, 3, -1, grads[4].shape[-1]).transpose(2, 0, 1, 3)
    if lax.axis_size("dp") * lax.axis_size("rows") > SHARDS:
        grads = [lax.psum_scatter(g, "rows", scatter_dimension=0, tiled=True) for g in grads]
    small = []
    for i in range(7):
        small += [norms[i].reshape(-1), norms[7 + i].reshape(-1)]
    return (*maps, *grads, *small)


def solution(mesh):
    split = P("rows", "dp", None, None)
    whole = P()
    shard = P(("dp", "rows"), None)
    shard_4 = P(("dp", "rows"), None, None, None)
    return jax.shard_map(
        on_device,
        mesh=mesh,
        in_specs=(split, split) + (whole,) * 22 + (split, split),
        out_specs=(split,) * 4
        + (shard, shard_4, shard, shard, shard_4, shard, shard)
        + (whole,) * 14,
        check_vma=False,
    )
```

time: 1380 us -> 211 us (0.15)
  waiting for transfers between devices: 564 us -> 0 us
  blocking collectives: 490 us -> 0 us
  Pallas kernels: 0 us -> 201 us
  matrix products: 127 us -> 0 us
  other arithmetic: 76.6 us -> 0 us
  local copies, waits for them, and re-layouts: 74.4 us -> 8.95 us
  between operations: 21.3 us -> 0.69 us
    reduce_scatter x11 -> x0, waiting for transfers between devices: 494 us -> none  [the longest x6 391 us: spread_grads(): lax.psum_scatter(shortened(grads), 'dp', scatter_dimension=0, tiled=True)]
    psum x12 -> x0, blocking collectives: 490 us -> none  [the longest x6 245 us: shared_grads(): return lax.psum((first, second), ('dp', 'rows'))]
    pallas_call x0 -> x2, Pallas kernels: none -> 201 us  [the longest x1 198 us: both_blocks(): pl.pallas_call(body, out_shape=parts[1], in_specs=spec_leaves[0], out_spe...]
    dot_general x133 -> x0, matrix products: 123 us -> none  [the longest x46 42.4 us: apply_matrix(): out = jnp.dot(flat, matrix, preferred_element_type=jnp.float32)]
    unnamed x17 -> x0, waiting for transfers between devices: 70.4 us -> none
    convert_element_type x34 -> x0, other arithmetic: 34.6 us -> none  [the longest x6 8.91 us: spread_grads(): part.astype(jnp.float32)]
    unnamed x558 -> x6, local copies, waits for them, and re-layouts: 38.2 us -> 8.95 us
    slice x40 -> x0, local copies, waits for them, and re-layouts: 15.9 us -> none  [the longest x8 3.22 us: rim_split(): pieces.append(flat[start:start + size].reshape(value.shape[1:]))]
  transfers between devices with their start and end apart: 20 -> 0, of which waited for: 13 -> 0; matrix products, arithmetic and copies ran while one was open for 6% -> 0% of each run, Pallas kernels for 0% -> 0%
where the time goes in v2:
time: 211 us; the launch traced here: 210 us
  Pallas kernels  201 us (95%)
  local copies, waits for them, and re-layouts  8.95 us (4%)
    pallas_call x1, Pallas kernels, both_blocks(): pl.pallas_call(body, out_shape=parts[1], in_specs=spec_leaves[0], out_spe...  198 us
    unnamed x6, local copies, waits for them, and re-layouts  8.95 us

profile of v2, /device:TPU:0, one launch (start us, length us, event | category | flops | bytes accessed | tf_op | source)
XLA Modules:
  0.0 210.4 jit_solution(4585551830861995660)
XLA Ops:
  0.7 2.0 copy.58
  2.7 2.8 %copy.57 = bf16[4,12,10,1024]{3,1,2,0:T(8,128)(2,1)} copy(bf16[4,12,10,1024]{3,0,2,1:T(4,128)(2,1)} %param.27) | data formatting | bytes 1966080 | tf_op args[1]
  5.5 198.0 %shard_map.441 = (f32[1,256]{1,0:T(1,128)}, f32[1,256]{1,0:T(1,128)}, f32[1,1024]{1,0:T(1,128)}, f32[1,512]{1,0:T(1,128)}, f32[1,512]{1,0:T(1,128)}, /*index=5*/...) custom-call(f32[1,256]{1,0:T(1,128)} %bitcast.85, ...), custom_call_target="tpu_custom_call" | custom-call | flops 16000000000 | bytes 30000000 | tf_op jit(solution)/shard_map/pallas_call | solution.py:1216
  203.6 0.0 copy-start
  203.6 2.8 %shard_map.442 = (bf16[2,7,4,2048]{3,2,1,0:T(4,128)(2,1)}, bf16[4,14,4,1024]{3,2,1,0:T(4,128)(2,1)}, f32[32,256]{1,0:T(8,128)}, f32[9,8,256]{2,1,0:T(8,128)}, f3...) custom-call(bf16[2,7,4,2048]{3,2,1,0:T(4,128)(2,1)} %get-tuple-eleme, ...), custom_call_target="tpu_custom_call" | custom-call | tf_op jit(solution)/shard_map/pallas_call | solution.py:1062
  206.3 2.4 %copy.53 = bf16[2,12,5,2048]{3,0,2,1:T(2,128)(2,1)} copy(bf16[2,12,5,2048]{3,1,2,0:T(8,128)(2,1)} %bitcast.55) | data formatting | bytes 983040
  208.7 0.0 copy-done
  208.7 1.7 copy.54
Async XLA Ops:
  203.6 5.2 %copy-start = (bf16[4,10,12,1024]{3,2,1,0:T(8,128)(2,1)S(1)}, bf16[4,10,12,1024]{3,2,1,0:T(8,128)(2,1)}, u32[]{:S(2)}) copy-start(bf16[4,10,12,1024]{3,2,1,0:T(8,128)(2,1)} %get-tuple-element.99) | copy-start | bytes 2949124

commit v3 on v2

--- a/solution.py
+++ b/solution.py
@@ -20,20 +20,43 @@
 EPS = 1e-05
 LEAF = 1024
 NARROW, SPATIAL, WIDENED, SQUEEZE, STRIDED, OUTPUT, SHORTCUT = range(7)
-NEAR = (0, 1, 2, 3, 4)
-FAR = (0, 2, 3, 4, 1)
+Y_FIRST = (0, 1, 2, 3, 4)
+X_FIRST = (0, 2, 1, 3, 4)
+Z_FIRST = (0, 3, 2, 1, 4)
 BITS = 5
 SHARDS = 1 << BITS
-G_REDUCE_ONE, G_SPATIAL_ONE, G_EXPAND_ONE, G_REDUCE_TWO, G_SPATIAL_TWO, G_EXPAND_TWO, G_SHORTCUT_TWO = range(7)
+REDUCE_ONE, SPATIAL_ONE, EXPAND_ONE, REDUCE_TWO, SPATIAL_TWO, EXPAND_TWO, SHORTCUT_TWO = range(7)
+(
+    G_REDUCE_ONE,
+    G_SPATIAL_ONE,
+    G_EXPAND_ONE,
+    G_REDUCE_TWO,
+    G_SPATIAL_TWO_0,
+    G_SPATIAL_TWO_1,
+    G_SPATIAL_TWO_2,
+    G_EXPAND_TWO_0,
+    G_EXPAND_TWO_1,
+    G_SHORTCUT_TWO_0,
+    G_SHORTCUT_TWO_1,
+    G_SHORTCUT_TWO_2,
+) = range(12)
 GRADS = (
-    (32, 256, NEAR),
-    (144, 128, FAR),
-    (16, 512, NEAR),
-    (32, 512, FAR),
-    (144, 512, NEAR),
-    (16, 2048, FAR),
-    (32, 2048, FAR),
+    (REDUCE_ONE, 32, 0, 0, 256, Y_FIRST),
+    (SPATIAL_ONE, 144, 0, 0, 128, Z_FIRST),
+    (EXPAND_ONE, 16, 0, 0, 512, Y_FIRST),
+    (REDUCE_TWO, 32, 0, 0, 512, Z_FIRST),
+    (SPATIAL_TWO, 48, 0, 0, 512, Y_FIRST),
+    (SPATIAL_TWO, 48, 1, 0, 512, X_FIRST),
+    (SPATIAL_TWO, 48, 2, 0, 512, Z_FIRST),
+    (EXPAND_TWO, 16, 0, 0, 1024, X_FIRST),
+    (EXPAND_TWO, 16, 0, 1024, 1024, Z_FIRST),
+    (SHORTCUT_TWO, 32, 0, 0, 768, Z_FIRST),
+    (SHORTCUT_TWO, 32, 0, 768, 640, Y_FIRST),
+    (SHORTCUT_TWO, 32, 0, 1408, 640, X_FIRST),
 )
+SPATIAL_TWO_PARTS = (G_SPATIAL_TWO_0, G_SPATIAL_TWO_1, G_SPATIAL_TWO_2)
+EXPAND_TWO_PARTS = (G_EXPAND_TWO_0, G_EXPAND_TWO_1)
+SHORTCUT_TWO_PARTS = (G_SHORTCUT_TWO_0, G_SHORTCUT_TWO_1, G_SHORTCUT_TWO_2)
 (
     AT_ONE,
     AT_TWO,
@@ -50,19 +73,19 @@
     AT_TWELVE,
 ) = range(13)
 SUMS = (
-    (2, 256),
-    (2, 256),
-    (2, 1024),
-    (2, 512),
-    (2, 512),
-    (2, 2048),
-    (2, 2048),
-    (3, 2048),
-    (2, 512),
-    (2, 512),
-    (2, 1024),
-    (2, 256),
-    (2, 256),
+    (2, 256, True),
+    (2, 256, True),
+    (2, 1024, False),
+    (2, 512, True),
+    (2, 512, True),
+    (2, 2048, False),
+    (2, 2048, False),
+    (3, 2048, False),
+    (2, 512, True),
+    (2, 512, True),
+    (2, 1024, True),
+    (2, 256, True),
+    (2, 256, True),
 )
 
 
@@ -267,7 +290,7 @@
 
 
     def place(self, name, shard):
-        order = GRADS[name][2]
+        order = GRADS[name][5]
         if isinstance(shard, int):
             return sum(((shard >> b) & 1) << (BITS - 1 - k) for k, b in enumerate(order))
         where = 0
@@ -276,7 +299,7 @@
         return where
 
     def halving(self, name, stage):
-        order = GRADS[name][2]
+        order = GRADS[name][5]
         start = 0
         for k in range(stage):
             start = start + bit_of(self.shard, order[k]) * (1 << (BITS - 1 - k))
@@ -291,11 +314,12 @@
         return start + mine * half, start + (1 - mine) * half, half, offset, partner
 
     def grad_copy(self, name, stage):
-        rows = GRADS[name][0]
+        array, rows, part, lane, lanes, _ = GRADS[name]
         _, away, half, offset, partner = self.halving(name, stage)
         index = name * BITS + stage
+        away = pl.ds(pl.multiple_of((part * SHARDS + away) * rows, 16), half * rows)
         return pltpu.make_async_remote_copy(
-            self.grads[name].at[pl.ds(pl.multiple_of(away * rows, 16), half * rows)],
+            self.grads[array].at[away, lane : lane + lanes],
             self.recv[name].at[pl.ds(offset * rows, half * rows)],
             self.grad_send.at[index],
             self.grad_recv.at[index],
@@ -306,11 +330,17 @@
     def grad_start(self, name):
         self.grad_copy(name, 0).start()
 
+    def grad_steps(self, stage, *names):
+        for name in names:
+            self.grad_step(name, stage)
+
     def grad_step(self, name, stage):
-        rows, lanes, _ = GRADS[name]
+        array, rows, part, lane, lanes, _ = GRADS[name]
         keep, _, half, offset, _ = self.halving(name, stage)
+        keep = part * SHARDS + keep
         self.grad_copy(name, stage).wait_recv()
-        own, came = self.grads[name], self.recv[name]
+        own, came = self.grads[array], self.recv[name]
+        across = slice(lane, lane + lanes)
         if stage < BITS - 1:
             height = 16
             while height * lanes < 32768 and (half * rows) % (2 * height) == 0:
@@ -319,24 +349,25 @@
             def add(step):
                 here = pl.ds(pl.multiple_of(keep * rows + step * height, 16), height)
                 there = pl.ds(pl.multiple_of(offset * rows + step * height, 16), height)
-                own[here, :] = (own[here, :].astype(F32) + came[there, :].astype(F32)).astype(BF16)
+                total = own[here, across].astype(F32) + came[there, :].astype(F32)
+                own[here, across] = total.astype(BF16)
 
             loop(half * rows // height, add)
             self.grad_copy(name, stage + 1).start()
             return
         here = pl.ds(pl.multiple_of(keep * rows, 16), rows)
         there = pl.ds(offset * rows, rows)
-        out = self.grad_out[name]
-        total = own[here, :].astype(F32) + came[there, :].astype(F32)
-        if name == G_SPATIAL_ONE:
+        out = self.grad_out[array]
+        total = own[here, across].astype(F32) + came[there, :].astype(F32)
+        if array == SPATIAL_ONE:
             for tap in range(9):
                 out[tap, :, 0:128] = total[tap * 16 : tap * 16 + 8]
                 out[tap, :, 128:256] = total[tap * 16 + 8 : tap * 16 + 16]
-        elif name == G_EXPAND_ONE:
+        elif array == EXPAND_ONE:
             out[:, 0:512] = total[0:8]
             out[:, 512:1024] = total[8:16]
         else:
-            out[...] = total
+            out[part * rows : part * rows + rows, across] = total
 
     def grads_sent(self):
         for name in range(len(GRADS)):
@@ -344,15 +375,13 @@
                 self.grad_copy(name, stage).wait_send()
 
     def grad_store(self, name, block, value, lanes=slice(None), row=0):
-        rows, _, _ = GRADS[name]
-        per = 16 if name == G_SPATIAL_TWO else rows
+        array, rows, part, _, _, _ = GRADS[name]
+        per = 16 if array == SPATIAL_TWO else rows
         count = 256 // per
-        base = self.place(name, block * count) * rows + row
+        base = (part * SHARDS + self.place(name, block * count)) * rows + row
         for s in range(count):
-            where = base + self.place(name, s) * rows
-            if not isinstance(where, int):
-                where = pl.multiple_of(where, 16)
-            self.grads[name][pl.ds(where, per), lanes] = value[s * per : (s + 1) * per].astype(BF16)
+            where = pl.multiple_of(base + self.place(name, s) * rows, 16)
+            self.grads[array][pl.ds(where, per), lanes] = value[s * per : (s + 1) * per].astype(BF16)
 
 
     def run(self):
@@ -721,8 +750,22 @@
         self.slope5[...] = value
         self.sum_start(AT_EIGHT, (col_sum(value), col_sum(value * self.off_mean(STRIDED, z5[...]))))
 
+        for name in EXPAND_TWO_PARTS:
+            first_lane = GRADS[name][3]
+
+            def grad_expand_two(step):
+                m, n = step // 2, lax.rem(step, 2)
+                left = h5[:, pl.ds(pl.multiple_of(m * 256, 256), 256)]
+                lanes = pl.ds(pl.multiple_of(first_lane + n * 512, 512), 512)
+                self.grad_store(name, m, mm_tn(left, dz6[:, lanes]), lanes)
+
+            loop(4, grad_expand_two)
+            self.grad_start(name)
+
         def clear(row):
             big[row] = jnp.zeros(big.shape[1:], F32)
+
+        loop(rows, clear)
 
         def shortcut_back(n):
             lanes = pl.ds(pl.multiple_of(n * 256, 256), 256)
@@ -730,26 +773,22 @@
             for o in range(rows // 2):
                 big[2 * o, 0:half, :, lanes] = value[o]
 
-        def grad_expand_two(step):
-            m, n = step // 4, lax.rem(step, 4)
-            left = h5[:, pl.ds(pl.multiple_of(m * 256, 256), 256)]
-            lanes = pl.ds(pl.multiple_of(n * 512, 512), 512)
-            self.grad_store(G_EXPAND_TWO, m, mm_tn(left, dz6[:, lanes]), lanes)
-
-        def grad_shortcut_two(step):
-            m, n = step // 4, lax.rem(step, 4)
+        loop(4, shortcut_back)
+
+        def grad_shortcut_two(m):
             here = pl.ds(pl.multiple_of(m * 256, 256), 256)
             left = jnp.concatenate(
                 [flat(feed[2 * o, 0:half, :, here]) for o in range(rows // 2)], axis=0
             )
-            lanes = pl.ds(pl.multiple_of(n * 512, 512), 512)
-            self.grad_store(G_SHORTCUT_TWO, m, mm_tn(left, dzs[:, lanes]), lanes)
-
-        loop(8, grad_expand_two)
-        self.grad_start(G_EXPAND_TWO)
+            for name in SHORTCUT_TWO_PARTS:
+                lanes = slice(GRADS[name][3], GRADS[name][3] + GRADS[name][4])
+                self.grad_store(name, m, mm_tn(left, dzs[:, lanes]), lanes)
+
+        loop(4, grad_shortcut_two)
+        for name in SHORTCUT_TWO_PARTS:
+            self.grad_start(name)
+        self.grad_steps(0, *EXPAND_TWO_PARTS)
         self.sum_turn(AT_EIGHT)
-        loop(rows, clear)
-        loop(4, shortcut_back)
         totals = self.sum_finish(AT_EIGHT)
         self.norm_back_ready(STRIDED, totals[0:1], totals[1:2], part(512))
         dz5 = self.dz5
@@ -761,10 +800,6 @@
         @pl.when(jnp.logical_not(first))
         def _():
             above.start()
-
-        loop(16, grad_shortcut_two)
-        self.grad_start(G_SHORTCUT_TWO)
-        self.grad_step(G_EXPAND_TWO, 0)
 
         dh4 = self.dh4
         for i in (1, 2, 0):
@@ -804,25 +839,23 @@
         sums = loop(rows * 2, slope_four, (nothing, nothing))
         self.sum_start(AT_NINE, sums)
         self.sum_turn(AT_NINE)
-        self.grad_step(G_SHORTCUT_TWO, 0)
-        self.grad_step(G_EXPAND_TWO, 1)
-        for j in range(3):
+        self.grad_steps(0, *SHORTCUT_TWO_PARTS)
+        self.grad_steps(1, *EXPAND_TWO_PARTS)
+
+        for i, name in enumerate(SPATIAL_TWO_PARTS):
 
             def grad_spatial_two(step):
-                i, m = step // 2, lax.rem(step, 2)
+                j, m = step // 2, lax.rem(step, 2)
                 here = pl.ds(pl.multiple_of(m * 256, 256), 256)
+                start = half * ((1 - j) * (2 - j) // 2) + (half + 1) * (j * (j + 1) // 2 - j)
                 left = jnp.concatenate(
-                    [
-                        flat(h4[2 * o + i, starts[j] : starts[j] + half, :, here])
-                        for o in range(rows // 2)
-                    ],
-                    axis=0,
+                    [flat(h4[2 * o + i, pl.ds(start, half), :, here]) for o in range(rows // 2)], axis=0
                 )
                 right = jnp.concatenate([flat(dz5[o, 0:half]) for o in range(rows // 2)], axis=0)
-                self.grad_store(G_SPATIAL_TWO, m, mm_tn(left, right), row=(i * 3 + j) * 16)
+                self.grad_store(name, m, mm_tn(left, right), row=j * 16)
 
             loop(6, grad_spatial_two)
-        self.grad_start(G_SPATIAL_TWO)
+            self.grad_start(name)
         totals = self.sum_finish(AT_NINE)
         self.norm_back_ready(SQUEEZE, totals[0:1], totals[1:2], full(512))
         dz4 = self.dz4
@@ -857,10 +890,9 @@
         sums = loop(rows, slope_three, ((nothing, nothing), (nothing, nothing)))
         sums = [jnp.concatenate([sums[0][i], sums[1][i]], axis=1) for i in range(2)]
         self.sum_start(AT_TEN, sums)
-        self.grad_step(G_SHORTCUT_TWO, 1)
         self.sum_turn(AT_TEN)
-        self.grad_step(G_SPATIAL_TWO, 0)
-        self.grad_step(G_EXPAND_TWO, 2)
+        self.grad_steps(0, *SPATIAL_TWO_PARTS)
+        self.grad_steps(2, *EXPAND_TWO_PARTS)
 
         def grad_reduce_two(m):
             here = pl.ds(pl.multiple_of(m * 256, 256), 256)
@@ -895,6 +927,9 @@
         sums = loop(rows, slope_spatial, (none, none))
         self.sum_start(AT_ELEVEN, sums)
         self.sum_turn(AT_ELEVEN)
+        self.grad_step(G_REDUCE_TWO, 0)
+        self.grad_steps(1, *SHORTCUT_TWO_PARTS)
+        self.grad_steps(3, *EXPAND_TWO_PARTS)
 
         left = h2[...].reshape(-1, 256)
         g_low = mm_tn(left, dz3[:, :, :, 0:512].reshape(-1, 512))
@@ -902,10 +937,8 @@
         for s in range(SHARDS):
             at = self.place(G_EXPAND_ONE, s) * 16
             piece = jnp.concatenate([g_low[s * 8 : s * 8 + 8], g_high[s * 8 : s * 8 + 8]], axis=0)
-            self.grads[G_EXPAND_ONE][at : at + 16, :] = piece.astype(BF16)
+            self.grads[EXPAND_ONE][at : at + 16, :] = piece.astype(BF16)
         self.grad_start(G_EXPAND_ONE)
-        self.grad_step(G_SPATIAL_TWO, 1)
-        self.grad_step(G_REDUCE_TWO, 0)
         totals = self.sum_finish(AT_ELEVEN)
         self.norm_back_ready(SPATIAL, totals[0:1], totals[1:2], full(256))
         dz2 = self.dz2
@@ -938,7 +971,7 @@
                     at = self.place(G_SPATIAL_ONE, s) * 144 + (i * 3 + j) * 16
                     piece = value[s * 8 : s * 8 + 8]
                     piece = jnp.concatenate([piece[:, 0:128], piece[:, 128:256]], axis=0)
-                    self.grads[G_SPATIAL_ONE][at : at + 16, :] = piece.astype(BF16)
+                    self.grads[SPATIAL_ONE][at : at + 16, :] = piece.astype(BF16)
         self.grad_start(G_SPATIAL_ONE)
 
         @pl.when(jnp.logical_not(last))
@@ -969,12 +1002,12 @@
         sums = loop(rows, slope_narrow, (none, none))
         self.sum_start(AT_TWELVE, sums)
         self.sum_turn(AT_TWELVE)
+        self.grad_step(G_SPATIAL_ONE, 0)
+        self.grad_steps(1, *SPATIAL_TWO_PARTS)
+        self.grad_steps(2, *SHORTCUT_TWO_PARTS)
         self.grad_step(G_EXPAND_ONE, 0)
-        self.grad_step(G_SPATIAL_ONE, 0)
-        self.grad_step(G_SHORTCUT_TWO, 2)
-        self.grad_step(G_SPATIAL_TWO, 2)
         self.grad_step(G_REDUCE_TWO, 1)
-        self.grad_step(G_EXPAND_TWO, 3)
+        self.grad_steps(4, *EXPAND_TWO_PARTS)
         totals = self.sum_finish(AT_TWELVE)
         self.norm_back_ready(NARROW, totals[0:1], totals[1:2], full(256))
         dz1 = h2
@@ -1008,30 +1041,26 @@
             copy = pltpu.make_async_copy(*pair, self.store_sem.at[2 + i])
             copy.start()
             stores.append(copy)
-        for name, stage in (
-            (G_EXPAND_ONE, 1),
-            (G_SPATIAL_ONE, 1),
-            (G_REDUCE_ONE, 0),
-            (G_SHORTCUT_TWO, 3),
-            (G_SPATIAL_TWO, 3),
-            (G_REDUCE_TWO, 2),
-            (G_EXPAND_TWO, 4),
-            (G_EXPAND_ONE, 2),
-            (G_SPATIAL_ONE, 2),
-            (G_REDUCE_ONE, 1),
-            (G_SHORTCUT_TWO, 4),
-            (G_SPATIAL_TWO, 4),
-            (G_REDUCE_TWO, 3),
-            (G_EXPAND_ONE, 3),
-            (G_SPATIAL_ONE, 3),
-            (G_REDUCE_ONE, 2),
-            (G_REDUCE_TWO, 4),
-            (G_EXPAND_ONE, 4),
-            (G_SPATIAL_ONE, 4),
-            (G_REDUCE_ONE, 3),
-            (G_REDUCE_ONE, 4),
-        ):
-            self.grad_step(name, stage)
+        self.grad_step(G_REDUCE_ONE, 0)
+        self.grad_step(G_SPATIAL_ONE, 1)
+        self.grad_step(G_EXPAND_ONE, 1)
+        self.grad_step(G_REDUCE_TWO, 2)
+        self.grad_steps(3, *SHORTCUT_TWO_PARTS)
+        self.grad_steps(2, *SPATIAL_TWO_PARTS)
+        self.grad_step(G_REDUCE_ONE, 1)
+        self.grad_step(G_SPATIAL_ONE, 2)
+        self.grad_step(G_EXPAND_ONE, 2)
+        self.grad_step(G_REDUCE_TWO, 3)
+        self.grad_steps(4, *SHORTCUT_TWO_PARTS)
+        self.grad_steps(3, *SPATIAL_TWO_PARTS)
+        self.grad_step(G_REDUCE_ONE, 2)
+        self.grad_step(G_SPATIAL_ONE, 3)
+        self.grad_step(G_EXPAND_ONE, 3)
+        self.grad_step(G_REDUCE_TWO, 4)
+        self.grad_steps(4, *SPATIAL_TWO_PARTS)
+        self.grad_step(G_REDUCE_ONE, 3)
+        self.grad_steps(4, G_SPATIAL_ONE, G_EXPAND_ONE)
+        self.grad_step(G_REDUCE_ONE, 4)
 
         for copy in stores:
             copy.wait()
@@ -1091,8 +1120,8 @@
         return vmem(value.shape, value.dtype)
 
     sums = []
-    for count, lanes in SUMS:
-        direct = lanes <= 512 and total <= 32
+    for count, lanes, straight in SUMS:
+        direct = straight and total <= 32
         sums.append(
             dict(
                 pay=vmem((count, lanes), F32),
@@ -1152,7 +1181,7 @@
         grad_send=dma((len(GRADS) * BITS,)),
         grad_recv=dma((len(GRADS) * BITS,)),
         coef=[vmem((8, gain.shape[1]), F32) for gain in gains],
-        recv=[vmem(((SHARDS - 1) * height, lanes), BF16) for height, lanes, _ in GRADS],
+        recv=[vmem(((SHARDS - 1) * height, lanes), BF16) for _, height, _, _, lanes, _ in GRADS],
         sums=sums,
     )
     grad_shapes = ((32, 256), (9, 8, 256), (8, 1024), (32, 512), (144, 512), (16, 2048), (32, 2048))

time: 211 us -> 170 us (0.81)
  Pallas kernels: 201 us -> 160 us
    pallas_call x1, Pallas kernels: 198 us -> 157 us  [both_blocks(): pl.pallas_call(body, out_shape=parts[1], in_specs=spec_leaves[0], out_spe...]
where the time goes in v3:
time: 170 us; the launch traced here: 169 us
  Pallas kernels  160 us (94%)
  local copies, waits for them, and re-layouts  8.95 us (5%)
    pallas_call x1, Pallas kernels, both_blocks(): pl.pallas_call(body, out_shape=parts[1], in_specs=spec_leaves[0], out_spe...  157 us
    unnamed x6, local copies, waits for them, and re-layouts  8.95 us

profile of v3, /device:TPU:0, one launch (start us, length us, event | category | flops | bytes accessed | tf_op | source)
XLA Modules:
  0.0 169.2 jit_solution(11061013991886226701)
XLA Ops:
  0.7 2.0 %copy.58 = bf16[2,12,5,2048]{3,1,2,0:T(8,128)(2,1)} copy(bf16[2,12,5,2048]{3,0,2,1:T(2,128)(2,1)} %param.51) | data formatting | bytes 983040 | tf_op args[25]
  2.7 2.8 %copy.57 = bf16[4,12,10,1024]{3,1,2,0:T(8,128)(2,1)} copy(bf16[4,12,10,1024]{3,0,2,1:T(4,128)(2,1)} %param.27) | data formatting | bytes 1966080 | tf_op args[1]
  5.5 156.8 %shard_map.441 = (f32[1,256]{1,0:T(1,128)}, f32[1,256]{1,0:T(1,128)}, f32[1,1024]{1,0:T(1,128)}, f32[1,512]{1,0:T(1,128)}, f32[1,512]{1,0:T(1,128)}, /*index=5*/...) custom-call(f32[1,256]{1,0:T(1,128)} %bitcast.85, ...), custom_call_target="tpu_custom_call" | custom-call | flops 16000000000 | bytes 30000000 | tf_op jit(solution)/shard_map/pallas_call | solution.py:1245
  162.3 0.0 copy-start
  162.3 2.8 %shard_map.442 = (bf16[2,7,4,2048]{3,2,1,0:T(4,128)(2,1)}, bf16[4,14,4,1024]{3,2,1,0:T(4,128)(2,1)}, f32[32,256]{1,0:T(8,128)}, f32[9,8,256]{2,1,0:T(8,128)}, f3...) custom-call(bf16[2,7,4,2048]{3,2,1,0:T(4,128)(2,1)} %get-tuple-eleme, ...), custom_call_target="tpu_custom_call" | custom-call | tf_op jit(solution)/shard_map/pallas_call | solution.py:1091
  165.1 2.4 %copy.53 = bf16[2,12,5,2048]{3,0,2,1:T(2,128)(2,1)} copy(bf16[2,12,5,2048]{3,1,2,0:T(8,128)(2,1)} %bitcast.55) | data formatting | bytes 983040
  167.5 0.0 copy-done
  167.5 1.7 %copy.54 = bf16[4,12,10,1024]{3,0,2,1:T(4,128)(2,1)} copy(bf16[4,12,10,1024]{3,1,2,0:T(8,128)(2,1)S(1)} %bitcast.53) | data formatting | bytes 1966080
Async XLA Ops:
  162.3 5.2 %copy-start = (bf16[4,10,12,1024]{3,2,1,0:T(8,128)(2,1)S(1)}, bf16[4,10,12,1024]{3,2,1,0:T(8,128)(2,1)}, u32[]{:S(2)}) copy-start(bf16[4,10,12,1024]{3,2,1,0:T(8,128)(2,1)} %get-tuple-element.99) | copy-start | bytes 2949124

commit v4 on v3

--- a/solution.py
+++ b/solution.py
@@ -80,10 +80,10 @@
     (2, 512, True),
     (2, 2048, False),
     (2, 2048, False),
-    (3, 2048, False),
+    (1, 6144, False),
     (2, 512, True),
     (2, 512, True),
-    (2, 1024, True),
+    (2, 1024, False),
     (2, 256, True),
     (2, 256, True),
 )
@@ -287,6 +287,29 @@
             device_id=(self.d, self.r + step),
             device_id_type=MESH,
         )
+
+    def has_strip(self, step):
+        return self.r > 0 if step < 0 else self.r < self.r_size - 1
+
+    def edge_send(self, step, value, stage, target, slot):
+        count = value.shape[0]
+        base = value[0, 0:1].astype(BF16)
+        stage[0:count] = (value - base.astype(F32)).astype(BF16)
+        stage[count] = jnp.broadcast_to(base.astype(F32), value.shape[1:]).astype(BF16)
+
+        @pl.when(self.has_strip(step))
+        def _():
+            self.to_strip(step, stage, target, slot).start()
+
+    def edge_sent(self, step, stage, target, slot):
+        @pl.when(self.has_strip(step))
+        def _():
+            self.to_strip(step, stage, target, slot).wait_send()
+
+    def edge_read(self, step, stage, target, slot):
+        self.to_strip(-step, stage, target, slot).wait_recv()
+        count = target.shape[0] - 1
+        return target[0:count].astype(F32) + target[count].astype(F32)[None]
 
 
     def place(self, name, shard):
@@ -436,7 +459,7 @@
         def part(lanes):
             return wide(self.half_count[...], lanes)
 
-        def make_mask(row):
+        def mask_of(row):
             place = lax.broadcasted_iota(jnp.int32, (cols, views, 128), 0)
             column = jnp.where(place < half, 2 * place, 2 * (place - half) + 1)
             view = lax.broadcasted_iota(jnp.int32, (cols, views, 128), 1)
@@ -445,9 +468,19 @@
             tall_b = jnp.where(where < HB, live_b, 0)
             in_a = (view < self.live_a) & (view < tall_a)
             in_b = (view >= self.live_a) & (view - self.live_a < tall_b) & (column < WB)
-            mask[row] = jnp.where(in_a | in_b, 1.0, 0.0).astype(F32)
+            return jnp.where(in_a | in_b, 1.0, 0.0).astype(F32)
+
+        def make_mask(row):
+            mask[row] = mask_of(row)
 
         loop(rows, make_mask)
+        side, side_2 = self.side, self.side_2
+        above_a, below_a, above_2, below_2 = (
+            self.edge_a.at[0],
+            self.edge_a.at[1],
+            self.edge_2.at[0],
+            self.edge_2.at[1],
+        )
 
         for ref in (h1, self.dz2):
             lanes = ref.shape[-1]
@@ -495,6 +528,8 @@
         self.greeted()
         self.sum_start(AT_ONE, sums)
         self.sum_turn(AT_ONE)
+        self.edge_send(-1, z1[0], side.at[0], below_a, 0)
+        self.edge_send(1, z1[rows - 1], side.at[1], above_a, 1)
         loads.ca.wait()
         loads.cb.wait()
         for o in range(rows // 2):
@@ -509,28 +544,25 @@
                     self.cot[h, o * half + p] = jnp.concatenate([near, rest], axis=0).astype(BF16)
         self.norm_ready(NARROW, self.sum_finish(AT_ONE), full(256))
 
+        def hidden_of(value, live):
+            value = self.act(NARROW, value)
+            return (value * sigmoid(value) * live).astype(BF16).reshape(cols, views, -1)
+
         def hidden_one(row):
-            value = self.act(NARROW, flat(z1[row]))
-            value = (value * sigmoid(value) * row_mask(row, 256)).astype(BF16)
-            value = value.reshape(cols, views, -1)
+            value = hidden_of(flat(z1[row]), row_mask(row, 256))
             for k in range(cols):
                 h1[row + 1, natural[k] + 1] = value[k]
 
-        first, last = self.r == 0, self.r == self.r_size - 1
-        hidden_one(0)
-        hidden_one(rows - 1)
-        up = self.to_strip(-1, h1.at[1], h1.at[rows + 1], 0)
-        down = self.to_strip(1, h1.at[rows], h1.at[0], 1)
-
-        @pl.when(jnp.logical_not(first))
-        def _():
-            up.start()
-
-        @pl.when(jnp.logical_not(last))
-        def _():
-            down.start()
-
-        loop(rows - 2, lambda i: hidden_one(i + 1))
+        loop(rows, hidden_one)
+
+        def hidden_edge(step, source, slot, row):
+            @pl.when(self.has_strip(step))
+            def _():
+                given = flat(self.edge_read(step, side.at[0], source, slot))
+                value = hidden_of(given, wide(flat(mask_of(row)), 256))
+                for k in range(cols):
+                    h1[row + 1, natural[k] + 1] = value[k]
+
         loads.w2.wait()
 
         def conv_row(row, carry):
@@ -548,17 +580,15 @@
 
         sums = loop(rows - 2, lambda i, carry: conv_row(i + 1, carry), (none, none))
 
-        @pl.when(jnp.logical_not(last))
-        def _():
-            self.to_strip(1, h1.at[rows], h1.at[rows + 1], 0).wait_recv()
-
-        @pl.when(jnp.logical_not(first))
-        def _():
-            self.to_strip(-1, h1.at[1], h1.at[0], 1).wait_recv()
-
+        hidden_edge(-1, above_a, 1, -1)
+        hidden_edge(1, below_a, 0, rows)
         sums = conv_row(rows - 1, conv_row(0, sums))
         self.sum_start(AT_TWO, sums)
         self.sum_turn(AT_TWO)
+        self.edge_sent(-1, side.at[0], below_a, 0)
+        self.edge_sent(1, side.at[1], above_a, 1)
+        self.edge_send(-1, z2[0], side.at[0], below_2, 2)
+        self.edge_send(1, z2[rows - 1], side.at[1], above_2, 3)
         loads.w3.wait()
         self.norm_ready(SPATIAL, self.sum_finish(AT_TWO), full(256))
 
@@ -606,6 +636,7 @@
         sums = loop(rows, squeeze_row, (nothing, nothing))
         self.sum_start(AT_FOUR, sums)
         self.sum_turn(AT_FOUR)
+        self.edge_send(1, z4[rows - 1], side_2, self.edge_4, 4)
 
         def even(ref):
             return jnp.concatenate([flat(ref[2 * o, 0:half]) for o in range(rows // 2)], axis=0)
@@ -631,14 +662,7 @@
                 start = p * (half + 1)
                 h4[row + 1, start : start + half] = value.astype(BF16).reshape(half, views, -1)
 
-        hidden_four(rows - 1)
-        below = self.to_strip(1, h4.at[rows], h4.at[0], 2)
-
-        @pl.when(jnp.logical_not(last))
-        def _():
-            below.start()
-
-        loop(rows - 1, hidden_four)
+        loop(rows, hidden_four)
         loads.w5.wait()
         starts = (half, 0, half + 1)
 
@@ -651,9 +675,16 @@
         for i in (1, 2, 0):
             if i == 0:
 
-                @pl.when(jnp.logical_not(first))
+                @pl.when(self.has_strip(-1))
                 def _():
-                    self.to_strip(-1, h4.at[rows], h4.at[0], 2).wait_recv()
+                    given = self.edge_read(-1, side_2, self.edge_4, 4)
+                    live = mask_of(-1)
+                    for p in range(2):
+                        here = slice(p * half, p * half + half)
+                        point = self.act(SQUEEZE, flat(given[here]))
+                        point = point * sigmoid(point) * wide(flat(live[here]), 512)
+                        start = p * (half + 1)
+                        h4[0, start : start + half] = point.astype(BF16).reshape(half, views, -1)
 
             for j in range(3):
                 tap = (i * 3 + j) * 512
@@ -667,6 +698,15 @@
         self.sum_start(AT_FIVE, (col_sum(kept), col_sum(kept * value)))
         self.sum_turn(AT_FIVE)
         self.sum_turn(AT_SHORT)
+        self.edge_sent(1, side_2, self.edge_4, 4)
+        row_5 = half * views
+        self.edge_send(
+            -1,
+            z5[0:row_5, :].reshape(half, views, -1),
+            side_2.at[0 : half + 1],
+            self.edge_5,
+            5,
+        )
         loads.w6.wait()
         self.norm_ready(STRIDED, self.sum_finish(AT_FIVE), part(512))
         value = self.act(STRIDED, z5[...])
@@ -688,7 +728,7 @@
         self.sum_turn(AT_SIX)
         self.norm_ready(OUTPUT, self.sum_finish(AT_SIX), part(2048))
 
-        top, cot = self.top, self.cot
+        dh4, cot = self.dh4, self.cot
         zero = jnp.zeros((1, LEAF), F32)
         for h in range(2):
             lanes = slice(h * LEAF, h * LEAF + LEAF)
@@ -702,7 +742,8 @@
                 given = flat(cot[h, here]).astype(F32)
                 slope = given * there * (sigma * (1.0 + value * (1.0 - sigma)))
                 cot[h, here] = (value * sigma * there).astype(BF16).reshape(2, views, -1)
-                top[h, here] = slope.reshape(2, views, -1)
+                for n in range(2):
+                    dh4[2 * h + n, here] = slope[:, n * 512 : n * 512 + 512].reshape(2, views, -1)
                 return (
                     carry[0] + col_sum(slope),
                     carry[1] + col_sum(slope * self.off_mean(OUTPUT, main, lanes)),
@@ -711,8 +752,9 @@
 
             sums = loop(half, out_step, (zero, zero, zero))
             for i in range(3):
-                self.top_sum[i : i + 1, lanes] = sums[i]
-        self.sum_start(AT_SEVEN, [self.top_sum[i : i + 1, :] for i in range(3)])
+                start = i * 2 * LEAF + h * LEAF
+                self.top_sum[:, start : start + LEAF] = sums[i]
+        self.sum_start(AT_SEVEN, [self.top_sum[...]])
         for o in range(rows // 2):
             for p in range(half):
                 for h in range(2):
@@ -729,8 +771,9 @@
             copy.start()
         self.sum_turn(AT_SEVEN)
         totals = self.sum_finish(AT_SEVEN)
-        self.norm_back_ready(OUTPUT, totals[0:1], totals[1:2], part(2048))
-        self.norm_back_ready(SHORTCUT, totals[0:1], totals[2:3], part(2048))
+        totals = [totals[:, i * 2 * LEAF : (i + 1) * 2 * LEAF] for i in range(3)]
+        self.norm_back_ready(OUTPUT, totals[0], totals[1], part(2048))
+        self.norm_back_ready(SHORTCUT, totals[0], totals[2], part(2048))
 
         dz6, dzs = self.dz6, self.dzs
         for h in range(2):
@@ -740,7 +783,7 @@
                 here = pl.ds(pair * 2, 2)
                 there = pl.ds(pl.multiple_of(pair * 2 * views, 16), 2 * views)
                 live = wide(self.half_mask[there, :], LEAF)
-                slope = flat(top[h, here])
+                slope = jnp.concatenate([flat(dh4[2 * h + n, here]) for n in range(2)], axis=1)
                 dz6[there, lanes] = self.back(OUTPUT, slope, flat(big[h, here]), live, lanes)
                 dzs[there, lanes] = self.back(SHORTCUT, slope, flat(big[2 + h, here]), live, lanes)
 
@@ -749,6 +792,16 @@
         value = mm_nt(dz6[...], self.w6[...]) * slope_of(self.act(STRIDED, z5[...]))
         self.slope5[...] = value
         self.sum_start(AT_EIGHT, (col_sum(value), col_sum(value * self.off_mean(STRIDED, z5[...]))))
+
+        self.edge_sent(-1, side_2.at[0 : half + 1], self.edge_5, 5)
+        edge_s = self.edge_4.at[0 : half + 1]
+        self.edge_send(
+            -1,
+            self.slope5[0:row_5, :].reshape(half, views, -1),
+            side_2.at[0 : half + 1],
+            edge_s,
+            6,
+        )
 
         for name in EXPAND_TWO_PARTS:
             first_lane = GRADS[name][3]
@@ -795,19 +848,16 @@
         value = self.back(STRIDED, self.slope5[...], z5[...], wide(self.half_mask[...], 512))
         for o in range(rows // 2):
             dz5[o, 0:half] = value[o * half * views : (o + 1) * half * views].reshape(half, views, -1)
-        above = self.to_strip(-1, dz5.at[0], dz5.at[rows // 2], 3)
-
-        @pl.when(jnp.logical_not(first))
-        def _():
-            above.start()
-
-        dh4 = self.dh4
         for i in (1, 2, 0):
             if i == 0:
 
-                @pl.when(jnp.logical_not(last))
+                @pl.when(self.has_strip(1))
                 def _():
-                    self.to_strip(1, dz5.at[0], dz5.at[rows // 2], 3).wait_recv()
+                    given = self.edge_read(1, side_2.at[0 : half + 1], edge_s, 6)
+                    point = self.edge_read(1, side_2.at[0 : half + 1], self.edge_5, 5)
+                    live = wide(flat(mask_of(rows)[0:half]), 512)
+                    point = self.back(STRIDED, flat(given), flat(point), live)
+                    dz5[rows // 2, 0:half] = point.reshape(half, views, -1)
 
             lead = 1 if i == 0 else 0
             for j in (1, 2, 0):
@@ -890,9 +940,6 @@
         sums = loop(rows, slope_three, ((nothing, nothing), (nothing, nothing)))
         sums = [jnp.concatenate([sums[0][i], sums[1][i]], axis=1) for i in range(2)]
         self.sum_start(AT_TEN, sums)
-        self.sum_turn(AT_TEN)
-        self.grad_steps(0, *SPATIAL_TWO_PARTS)
-        self.grad_steps(2, *EXPAND_TWO_PARTS)
 
         def grad_reduce_two(m):
             here = pl.ds(pl.multiple_of(m * 256, 256), 256)
@@ -901,6 +948,9 @@
 
         loop(4, grad_reduce_two)
         self.grad_start(G_REDUCE_TWO)
+        self.sum_turn(AT_TEN)
+        self.grad_steps(0, *SPATIAL_TWO_PARTS)
+        self.grad_steps(2, *EXPAND_TWO_PARTS)
         totals = self.sum_finish(AT_TEN)
         self.norm_back_ready(WIDENED, totals[0:1], totals[1:2], full(1024))
         dz3 = feed
@@ -927,6 +977,10 @@
         sums = loop(rows, slope_spatial, (none, none))
         self.sum_start(AT_ELEVEN, sums)
         self.sum_turn(AT_ELEVEN)
+        self.edge_sent(-1, side.at[0], below_2, 2)
+        self.edge_sent(1, side.at[1], above_2, 3)
+        self.edge_send(-1, dh4[0, :, :, 0:256], side.at[0], below_a, 7)
+        self.edge_send(1, dh4[rows - 1, :, :, 0:256], side.at[1], above_a, 8)
         self.grad_step(G_REDUCE_TWO, 0)
         self.grad_steps(1, *SHORTCUT_TWO_PARTS)
         self.grad_steps(3, *EXPAND_TWO_PARTS)
@@ -949,20 +1003,7 @@
             for k in range(cols):
                 dz2[row + 1, natural[k] + 1] = value[k]
 
-        back_two(0)
-        back_two(rows - 1)
-        up = self.to_strip(-1, dz2.at[1], dz2.at[rows + 1], 4)
-        down = self.to_strip(1, dz2.at[rows], dz2.at[0], 5)
-
-        @pl.when(jnp.logical_not(first))
-        def _():
-            up.start()
-
-        @pl.when(jnp.logical_not(last))
-        def _():
-            down.start()
-
-        loop(rows - 2, lambda i: back_two(i + 1))
+        loop(rows, back_two)
         for i in range(3):
             for j in range(3):
                 left = h1[i : i + rows, j : j + cols].reshape(-1, 256)
@@ -974,13 +1015,18 @@
                     self.grads[SPATIAL_ONE][at : at + 16, :] = piece.astype(BF16)
         self.grad_start(G_SPATIAL_ONE)
 
-        @pl.when(jnp.logical_not(last))
-        def _():
-            self.to_strip(1, dz2.at[rows], dz2.at[rows + 1], 4).wait_recv()
-
-        @pl.when(jnp.logical_not(first))
-        def _():
-            self.to_strip(-1, dz2.at[1], dz2.at[0], 5).wait_recv()
+        def edge_two(step, slope_from, slope_slot, value_from, value_slot, row):
+            @pl.when(self.has_strip(step))
+            def _():
+                given = flat(self.edge_read(step, side.at[0], slope_from, slope_slot))
+                point = flat(self.edge_read(step, side.at[0], value_from, value_slot))
+                value = self.back(SPATIAL, given, point, wide(flat(mask_of(row)), 256))
+                value = value.reshape(cols, views, -1)
+                for k in range(cols):
+                    dz2[row + 1, natural[k] + 1] = value[k]
+
+        edge_two(-1, above_a, 8, above_2, 3, -1)
+        edge_two(1, below_a, 7, below_2, 2, rows)
 
         def slope_narrow(row, carry):
             value = 0.0
@@ -1067,17 +1113,9 @@
         self.sums_sent()
         self.grads_sent()
 
-        @pl.when(jnp.logical_not(first))
-        def _():
-            self.to_strip(-1, h1.at[1], h1.at[rows + 1], 0).wait_send()
-            self.to_strip(-1, dz5.at[0], dz5.at[rows // 2], 3).wait_send()
-            self.to_strip(-1, dz2.at[1], dz2.at[rows + 1], 4).wait_send()
-
-        @pl.when(jnp.logical_not(last))
-        def _():
-            self.to_strip(1, h1.at[rows], h1.at[0], 1).wait_send()
-            self.to_strip(1, h4.at[rows], h4.at[0], 2).wait_send()
-            self.to_strip(1, dz2.at[rows], dz2.at[0], 5).wait_send()
+        self.edge_sent(-1, side_2.at[0 : half + 1], edge_s, 6)
+        self.edge_sent(-1, side.at[0], below_a, 7)
+        self.edge_sent(1, side.at[1], above_a, 8)
 
 
 def settle(*refs):
@@ -1161,10 +1199,9 @@
         h4=vmem((rows + 1, cols + 1, views, c_mid2), BF16),
         h5=vmem((pixels, c_mid2), BF16),
         big=full(c_in, F32),
-        top=vmem((2, cols, views, LEAF), F32),
         short_sum=vmem((2, c_out), F32),
         main_sum=vmem((2, c_out), F32),
-        top_sum=vmem((3, c_out), F32),
+        top_sum=vmem((1, 3 * c_out), F32),
         dz6=vmem((pixels, c_out), BF16),
         dzs=vmem((pixels, c_out), BF16),
         slope5=vmem((pixels, c_mid2), F32),
@@ -1176,8 +1213,14 @@
         g3=vmem((SHARDS * 16, 512), BF16),
         load_sem=dma((11,)),
         store_sem=dma((4,)),
-        halo_send=dma((6,)),
-        halo_recv=dma((6,)),
+        side=vmem((2, cols + 1, views, c_mid), BF16),
+        edge_a=vmem((2, cols + 1, views, c_mid), BF16),
+        edge_2=vmem((2, cols + 1, views, c_mid), BF16),
+        side_2=vmem((cols + 1, views, c_mid2), BF16),
+        edge_4=vmem((cols + 1, views, c_mid2), BF16),
+        edge_5=vmem((half + 1, views, c_mid2), BF16),
+        halo_send=dma((9,)),
+        halo_recv=dma((9,)),
         grad_send=dma((len(GRADS) * BITS,)),
         grad_recv=dma((len(GRADS) * BITS,)),
         coef=[vmem((8, gain.shape[1]), F32) for gain in gains],

time: 170 us -> 166 us (0.976)
  Pallas kernels: 160 us -> 156 us
    pallas_call x1, Pallas kernels: 157 us -> 153 us  [both_blocks(): pl.pallas_call(body, out_shape=parts[1], in_specs=spec_leaves[0], out_spe...]
where the time goes in v4:
time: 166 us
  Pallas kernels  156 us (94%)
  local copies, waits for them, and re-layouts  8.95 us (5%)
    pallas_call x1, Pallas kernels, both_blocks(): pl.pallas_call(body, out_shape=parts[1], in_specs=spec_leaves[0], out_spe...  153 us
    unnamed x6, local copies, waits for them, and re-layouts  8.95 us

profile of v4, /device:TPU:0, one launch (start us, length us, event | category | flops | bytes accessed | tf_op | source)
XLA Modules:
  0.0 165.5 jit_solution(4822035177330251455)
XLA Ops:
  0.7 2.0 %copy.58 = bf16[2,12,5,2048]{3,1,2,0:T(8,128)(2,1)} copy(bf16[2,12,5,2048]{3,0,2,1:T(2,128)(2,1)} %param.51) | data formatting | bytes 983040 | tf_op args[25]
  2.7 2.8 %copy.57 = bf16[4,12,10,1024]{3,1,2,0:T(8,128)(2,1)} copy(bf16[4,12,10,1024]{3,0,2,1:T(4,128)(2,1)} %param.27) | data formatting | bytes 1966080 | tf_op args[1]
  5.5 153.1 %shard_map.441 = (f32[1,256]{1,0:T(1,128)}, f32[1,256]{1,0:T(1,128)}, f32[1,1024]{1,0:T(1,128)}, f32[1,512]{1,0:T(1,128)}, f32[1,512]{1,0:T(1,128)}, /*index=5*/...) custom-call(f32[1,256]{1,0:T(1,128)} %bitcast.85, ...), custom_call_target="tpu_custom_call" | custom-call | flops 16000000000 | bytes 30000000 | tf_op jit(solution)/shard_map/pallas_call | solution.py:1288
  158.7 0.0 copy-start
  158.7 2.8 %shard_map.442 = (bf16[2,7,4,2048]{3,2,1,0:T(4,128)(2,1)}, bf16[4,14,4,1024]{3,2,1,0:T(4,128)(2,1)}, f32[32,256]{1,0:T(8,128)}, f32[9,8,256]{2,1,0:T(8,128)}, f3...) custom-call(bf16[2,7,4,2048]{3,2,1,0:T(4,128)(2,1)} %get-tuple-eleme, ...), custom_call_target="tpu_custom_call" | custom-call | tf_op jit(solution)/shard_map/pallas_call | solution.py:1129
  161.4 2.4 %copy.53 = bf16[2,12,5,2048]{3,0,2,1:T(2,128)(2,1)} copy(bf16[2,12,5,2048]{3,1,2,0:T(8,128)(2,1)} %bitcast.55) | data formatting | bytes 983040
  163.8 0.0 copy-done
  163.8 1.7 %copy.54 = bf16[4,12,10,1024]{3,0,2,1:T(4,128)(2,1)} copy(bf16[4,12,10,1024]{3,1,2,0:T(8,128)(2,1)S(1)} %bitcast.53) | data formatting | bytes 1966080
Async XLA Ops:
  158.7 5.2 %copy-start = (bf16[4,10,12,1024]{3,2,1,0:T(8,128)(2,1)S(1)}, bf16[4,10,12,1024]{3,2,1,0:T(8,128)(2,1)}, u32[]{:S(2)}) copy-start(bf16[4,10,12,1024]{3,2,1,0:T(8,128)(2,1)} %get-tuple-element.99) | copy-start | bytes 2949124

commit v5 on v4

--- a/solution.py
+++ b/solution.py
@@ -54,6 +54,23 @@
     (SHORTCUT_TWO, 32, 0, 768, 640, Y_FIRST),
     (SHORTCUT_TWO, 32, 0, 1408, 640, X_FIRST),
 )
+SLOTS = (
+    ((7, 0), (8, 0),),
+    (),
+    ((9, 0), (10, 0), (11, 0), (7, 1), (8, 1),),
+    (),
+    (),
+    (),
+    ((4, 0), (5, 0), (6, 0), (7, 2), (8, 2),),
+    (),
+    ((3, 0), (9, 1), (10, 1), (11, 1), (7, 3), (8, 3),),
+    (),
+    ((4, 1), (5, 1), (6, 1),),
+    (),
+    ((1, 0), (9, 2), (10, 2), (11, 2), (2, 0), (3, 1), (7, 4), (8, 4),),
+    (),
+    ((0, 0), (9, 3), (10, 3), (11, 3), (3, 2), (4, 2), (5, 2), (6, 2), (1, 1), (2, 1), (0, 1), (9, 4), (10, 4), (11, 4), (3, 3), (4, 3), (5, 3), (6, 3), (1, 2), (2, 2), (0, 2), (3, 4), (4, 4), (5, 4), (6, 4), (1, 3), (2, 3), (0, 3), (1, 4), (2, 4), (0, 4),),
+)
 SPATIAL_TWO_PARTS = (G_SPATIAL_TWO_0, G_SPATIAL_TWO_1, G_SPATIAL_TWO_2)
 EXPAND_TWO_PARTS = (G_EXPAND_TWO_0, G_EXPAND_TWO_1)
 SHORTCUT_TWO_PARTS = (G_SHORTCUT_TWO_0, G_SHORTCUT_TWO_1, G_SHORTCUT_TWO_2)
@@ -353,8 +370,8 @@
     def grad_start(self, name):
         self.grad_copy(name, 0).start()
 
-    def grad_steps(self, stage, *names):
-        for name in names:
+    def grad_slot(self, slot):
+        for name, stage in SLOTS[slot]:
             self.grad_step(name, stage)
 
     def grad_step(self, name, stage):
@@ -366,14 +383,13 @@
         across = slice(lane, lane + lanes)
         if stage < BITS - 1:
             height = 16
-            while height * lanes < 32768 and (half * rows) % (2 * height) == 0:
+            while height * lanes < 65536 and (half * rows) % (2 * height) == 0:
                 height *= 2
 
             def add(step):
                 here = pl.ds(pl.multiple_of(keep * rows + step * height, 16), height)
                 there = pl.ds(pl.multiple_of(offset * rows + step * height, 16), height)
-                total = own[here, across].astype(F32) + came[there, :].astype(F32)
-                own[here, across] = total.astype(BF16)
+                own[here, across] = own[here, across] + came[there, :]
 
             loop(half * rows // height, add)
             self.grad_copy(name, stage + 1).start()
@@ -840,7 +856,7 @@
         loop(4, grad_shortcut_two)
         for name in SHORTCUT_TWO_PARTS:
             self.grad_start(name)
-        self.grad_steps(0, *EXPAND_TWO_PARTS)
+        self.grad_slot(0)
         self.sum_turn(AT_EIGHT)
         totals = self.sum_finish(AT_EIGHT)
         self.norm_back_ready(STRIDED, totals[0:1], totals[1:2], part(512))
@@ -848,6 +864,7 @@
         value = self.back(STRIDED, self.slope5[...], z5[...], wide(self.half_mask[...], 512))
         for o in range(rows // 2):
             dz5[o, 0:half] = value[o * half * views : (o + 1) * half * views].reshape(half, views, -1)
+        self.grad_slot(1)
         for i in (1, 2, 0):
             if i == 0:
 
@@ -889,8 +906,7 @@
         sums = loop(rows * 2, slope_four, (nothing, nothing))
         self.sum_start(AT_NINE, sums)
         self.sum_turn(AT_NINE)
-        self.grad_steps(0, *SHORTCUT_TWO_PARTS)
-        self.grad_steps(1, *EXPAND_TWO_PARTS)
+        self.grad_slot(2)
 
         for i, name in enumerate(SPATIAL_TWO_PARTS):
 
@@ -906,6 +922,7 @@
 
             loop(6, grad_spatial_two)
             self.grad_start(name)
+        self.grad_slot(3)
         totals = self.sum_finish(AT_NINE)
         self.norm_back_ready(SQUEEZE, totals[0:1], totals[1:2], full(512))
         dz4 = self.dz4
@@ -919,6 +936,7 @@
             dz4[row, here] = value.reshape(half, views, -1)
 
         loop(rows * 2, back_four)
+        self.grad_slot(4)
 
         def slope_three(row, carry):
             done = []
@@ -940,6 +958,7 @@
         sums = loop(rows, slope_three, ((nothing, nothing), (nothing, nothing)))
         sums = [jnp.concatenate([sums[0][i], sums[1][i]], axis=1) for i in range(2)]
         self.sum_start(AT_TEN, sums)
+        self.grad_slot(5)
 
         def grad_reduce_two(m):
             here = pl.ds(pl.multiple_of(m * 256, 256), 256)
@@ -949,8 +968,7 @@
         loop(4, grad_reduce_two)
         self.grad_start(G_REDUCE_TWO)
         self.sum_turn(AT_TEN)
-        self.grad_steps(0, *SPATIAL_TWO_PARTS)
-        self.grad_steps(2, *EXPAND_TWO_PARTS)
+        self.grad_slot(6)
         totals = self.sum_finish(AT_TEN)
         self.norm_back_ready(WIDENED, totals[0:1], totals[1:2], full(1024))
         dz3 = feed
@@ -963,6 +981,7 @@
             dz3[row, here] = value.reshape(2, views, -1)
 
         loop(rows * half, back_three)
+        self.grad_slot(7)
 
 
         def slope_spatial(row, carry):
@@ -981,9 +1000,7 @@
         self.edge_sent(1, side.at[1], above_2, 3)
         self.edge_send(-1, dh4[0, :, :, 0:256], side.at[0], below_a, 7)
         self.edge_send(1, dh4[rows - 1, :, :, 0:256], side.at[1], above_a, 8)
-        self.grad_step(G_REDUCE_TWO, 0)
-        self.grad_steps(1, *SHORTCUT_TWO_PARTS)
-        self.grad_steps(3, *EXPAND_TWO_PARTS)
+        self.grad_slot(8)
 
         left = h2[...].reshape(-1, 256)
         g_low = mm_tn(left, dz3[:, :, :, 0:512].reshape(-1, 512))
@@ -993,6 +1010,7 @@
             piece = jnp.concatenate([g_low[s * 8 : s * 8 + 8], g_high[s * 8 : s * 8 + 8]], axis=0)
             self.grads[EXPAND_ONE][at : at + 16, :] = piece.astype(BF16)
         self.grad_start(G_EXPAND_ONE)
+        self.grad_slot(9)
         totals = self.sum_finish(AT_ELEVEN)
         self.norm_back_ready(SPATIAL, totals[0:1], totals[1:2], full(256))
         dz2 = self.dz2
@@ -1004,6 +1022,7 @@
                 dz2[row + 1, natural[k] + 1] = value[k]
 
         loop(rows, back_two)
+        self.grad_slot(10)
         for i in range(3):
             for j in range(3):
                 left = h1[i : i + rows, j : j + cols].reshape(-1, 256)
@@ -1014,6 +1033,7 @@
                     piece = jnp.concatenate([piece[:, 0:128], piece[:, 128:256]], axis=0)
                     self.grads[SPATIAL_ONE][at : at + 16, :] = piece.astype(BF16)
         self.grad_start(G_SPATIAL_ONE)
+        self.grad_slot(11)
 
         def edge_two(step, slope_from, slope_slot, value_from, value_slot, row):
             @pl.when(self.has_strip(step))
@@ -1048,12 +1068,7 @@
         sums = loop(rows, slope_narrow, (none, none))
         self.sum_start(AT_TWELVE, sums)
         self.sum_turn(AT_TWELVE)
-        self.grad_step(G_SPATIAL_ONE, 0)
-        self.grad_steps(1, *SPATIAL_TWO_PARTS)
-        self.grad_steps(2, *SHORTCUT_TWO_PARTS)
-        self.grad_step(G_EXPAND_ONE, 0)
-        self.grad_step(G_REDUCE_TWO, 1)
-        self.grad_steps(4, *EXPAND_TWO_PARTS)
+        self.grad_slot(12)
         totals = self.sum_finish(AT_TWELVE)
         self.norm_back_ready(NARROW, totals[0:1], totals[1:2], full(256))
         dz1 = h2
@@ -1071,6 +1086,7 @@
 
         loop(4, grad_reduce_one)
         self.grad_start(G_REDUCE_ONE)
+        self.grad_slot(13)
 
         def input_row(row):
             for n in range(2):
@@ -1087,27 +1103,8 @@
             copy = pltpu.make_async_copy(*pair, self.store_sem.at[2 + i])
             copy.start()
             stores.append(copy)
-        self.grad_step(G_REDUCE_ONE, 0)
-        self.grad_step(G_SPATIAL_ONE, 1)
-        self.grad_step(G_EXPAND_ONE, 1)
-        self.grad_step(G_REDUCE_TWO, 2)
-        self.grad_steps(3, *SHORTCUT_TWO_PARTS)
-        self.grad_steps(2, *SPATIAL_TWO_PARTS)
-        self.grad_step(G_REDUCE_ONE, 1)
-        self.grad_step(G_SPATIAL_ONE, 2)
-        self.grad_step(G_EXPAND_ONE, 2)
-        self.grad_step(G_REDUCE_TWO, 3)
-        self.grad_steps(4, *SHORTCUT_TWO_PARTS)
-        self.grad_steps(3, *SPATIAL_TWO_PARTS)
-        self.grad_step(G_REDUCE_ONE, 2)
-        self.grad_step(G_SPATIAL_ONE, 3)
-        self.grad_step(G_EXPAND_ONE, 3)
-        self.grad_step(G_REDUCE_TWO, 4)
-        self.grad_steps(4, *SPATIAL_TWO_PARTS)
-        self.grad_step(G_REDUCE_ONE, 3)
-        self.grad_steps(4, G_SPATIAL_ONE, G_EXPAND_ONE)
-        self.grad_step(G_REDUCE_ONE, 4)
-
+
+        self.grad_slot(14)
         for copy in stores:
             copy.wait()
         self.sums_sent()

time: 166 us -> 163 us (0.982)
  Pallas kernels: 156 us -> 153 us
    pallas_call x1, Pallas kernels: 153 us -> 150 us  [both_blocks(): pl.pallas_call(body, out_shape=parts[1], in_specs=spec_leaves[0], out_spe...]
where the time goes in v5:
time: 163 us; the launch traced here: 162 us
  Pallas kernels  153 us (94%)
  local copies, waits for them, and re-layouts  8.95 us (5%)
    pallas_call x1, Pallas kernels, both_blocks(): pl.pallas_call(body, out_shape=parts[1], in_specs=spec_leaves[0], out_spe...  150 us
    unnamed x6, local copies, waits for them, and re-layouts  8.95 us

profile of v5, /device:TPU:0, one launch (start us, length us, event | category | flops | bytes accessed | tf_op | source)
XLA Modules:
  0.0 162.4 jit_solution(16946547832359419148)
XLA Ops:
  0.7 2.0 %copy.58 = bf16[2,12,5,2048]{3,1,2,0:T(8,128)(2,1)} copy(bf16[2,12,5,2048]{3,0,2,1:T(2,128)(2,1)} %param.51) | data formatting | bytes 983040 | tf_op args[25]
  2.7 2.8 %copy.57 = bf16[4,12,10,1024]{3,1,2,0:T(8,128)(2,1)} copy(bf16[4,12,10,1024]{3,0,2,1:T(4,128)(2,1)} %param.27) | data formatting | bytes 1966080 | tf_op args[1]
  5.5 150.0 %shard_map.441 = (f32[1,256]{1,0:T(1,128)}, f32[1,256]{1,0:T(1,128)}, f32[1,1024]{1,0:T(1,128)}, f32[1,512]{1,0:T(1,128)}, f32[1,512]{1,0:T(1,128)}, /*index=5*/...) custom-call(f32[1,256]{1,0:T(1,128)} %bitcast.85, ...), custom_call_target="tpu_custom_call" | custom-call | flops 16000000000 | bytes 30000000 | tf_op jit(solution)/shard_map/pallas_call | solution.py:1285
  155.5 0.0 copy-start
  155.5 2.8 %shard_map.442 = (bf16[2,7,4,2048]{3,2,1,0:T(4,128)(2,1)}, bf16[4,14,4,1024]{3,2,1,0:T(4,128)(2,1)}, f32[32,256]{1,0:T(8,128)}, f32[9,8,256]{2,1,0:T(8,128)}, f3...) custom-call(bf16[2,7,4,2048]{3,2,1,0:T(4,128)(2,1)} %get-tuple-eleme, ...), custom_call_target="tpu_custom_call" | custom-call | tf_op jit(solution)/shard_map/pallas_call | solution.py:1126
  158.3 2.4 %copy.53 = bf16[2,12,5,2048]{3,0,2,1:T(2,128)(2,1)} copy(bf16[2,12,5,2048]{3,1,2,0:T(8,128)(2,1)} %bitcast.55) | data formatting | bytes 983040
  160.7 0.0 copy-done
  160.7 1.7 %copy.54 = bf16[4,12,10,1024]{3,0,2,1:T(4,128)(2,1)} copy(bf16[4,12,10,1024]{3,1,2,0:T(8,128)(2,1)S(1)} %bitcast.53) | data formatting | bytes 1966080
Async XLA Ops:
  155.5 5.2 %copy-start = (bf16[4,10,12,1024]{3,2,1,0:T(8,128)(2,1)S(1)}, bf16[4,10,12,1024]{3,2,1,0:T(8,128)(2,1)}, u32[]{:S(2)}) copy-start(bf16[4,10,12,1024]{3,2,1,0:T(8,128)(2,1)} %get-tuple-element.99) | copy-start | bytes 2949124

commit v6 on v5

--- a/solution.py
+++ b/solution.py
@@ -831,11 +831,6 @@
             loop(4, grad_expand_two)
             self.grad_start(name)
 
-        def clear(row):
-            big[row] = jnp.zeros(big.shape[1:], F32)
-
-        loop(rows, clear)
-
         def shortcut_back(n):
             lanes = pl.ds(pl.multiple_of(n * 256, 256), 256)
             value = mm_nt(dzs[...], self.ws[lanes, :]).reshape(rows // 2, half, views, -1)
@@ -938,12 +933,16 @@
         loop(rows * 2, back_four)
         self.grad_slot(4)
 
-        def slope_three(row, carry):
+        def slope_three(row, carry, even):
             done = []
             for n in range(2):
                 lanes = slice(n * 512, n * 512 + 512)
                 before = flat(z3[row, :, :, lanes])
-                grad = mm_nt(flat(dz4[row]), self.w4[lanes, :]) + flat(big[row, :, :, lanes])
+                grad = mm_nt(flat(dz4[row]), self.w4[lanes, :])
+                if even:
+                    count = half * views
+                    more = flat(big[row, 0:half, :, lanes])
+                    grad = jnp.concatenate([grad[:count] + more, grad[count:]], axis=0)
                 point = self.act(WIDENED, before, lanes) + flat(x[row, :, :, lanes]).astype(F32)
                 value = grad * slope_of(point)
                 big[row, :, :, lanes] = value.reshape(cols, views, -1)
@@ -955,7 +954,10 @@
                 )
             return tuple(done)
 
-        sums = loop(rows, slope_three, ((nothing, nothing), (nothing, nothing)))
+        def slope_pair(o, carry):
+            return slope_three(2 * o + 1, slope_three(2 * o, carry, True), False)
+
+        sums = loop(rows // 2, slope_pair, ((nothing, nothing), (nothing, nothing)))
         sums = [jnp.concatenate([sums[0][i], sums[1][i]], axis=1) for i in range(2)]
         self.sum_start(AT_TEN, sums)
         self.grad_slot(5)

time: 163 us -> 162 us (level)
  no operation moved by 1% of the time
where the time goes in v6:
time: 162 us
  Pallas kernels  152 us (94%)
  local copies, waits for them, and re-layouts  8.95 us (6%)
    pallas_call x1, Pallas kernels, both_blocks(): pl.pallas_call(body, out_shape=parts[1], in_specs=spec_leaves[0], out_spe...  149 us
    unnamed x6, local copies, waits for them, and re-layouts  8.95 us

profile of v6, /device:TPU:0, one launch (start us, length us, event | category | flops | bytes accessed | tf_op | source)
XLA Modules:
  0.0 161.7 jit_solution(16609195346756808544)
XLA Ops:
  0.7 2.0 %copy.58 = bf16[2,12,5,2048]{3,1,2,0:T(8,128)(2,1)} copy(bf16[2,12,5,2048]{3,0,2,1:T(2,128)(2,1)} %param.51) | data formatting | bytes 983040 | tf_op args[25]
  2.7 2.8 %copy.57 = bf16[4,12,10,1024]{3,1,2,0:T(8,128)(2,1)} copy(bf16[4,12,10,1024]{3,0,2,1:T(4,128)(2,1)} %param.27) | data formatting | bytes 1966080 | tf_op args[1]
  5.5 149.3 %shard_map.441 = (f32[1,256]{1,0:T(1,128)}, f32[1,256]{1,0:T(1,128)}, f32[1,1024]{1,0:T(1,128)}, f32[1,512]{1,0:T(1,128)}, f32[1,512]{1,0:T(1,128)}, /*index=5*/...) custom-call(f32[1,256]{1,0:T(1,128)} %bitcast.85, ...), custom_call_target="tpu_custom_call" | custom-call | flops 16000000000 | bytes 30000000 | tf_op jit(solution)/shard_map/pallas_call | solution.py:1287
  154.8 0.0 copy-start
  154.8 2.8 %shard_map.442 = (bf16[2,7,4,2048]{3,2,1,0:T(4,128)(2,1)}, bf16[4,14,4,1024]{3,2,1,0:T(4,128)(2,1)}, f32[32,256]{1,0:T(8,128)}, f32[9,8,256]{2,1,0:T(8,128)}, f3...) custom-call(bf16[2,7,4,2048]{3,2,1,0:T(4,128)(2,1)} %get-tuple-eleme, ...), custom_call_target="tpu_custom_call" | custom-call | tf_op jit(solution)/shard_map/pallas_call | solution.py:1128
  157.6 2.4 %copy.53 = bf16[2,12,5,2048]{3,0,2,1:T(2,128)(2,1)} copy(bf16[2,12,5,2048]{3,1,2,0:T(8,128)(2,1)} %bitcast.55) | data formatting | bytes 983040
  160.0 0.0 copy-done
  160.0 1.7 %copy.54 = bf16[4,12,10,1024]{3,0,2,1:T(4,128)(2,1)} copy(bf16[4,12,10,1024]{3,1,2,0:T(8,128)(2,1)S(1)} %bitcast.53) | data formatting | bytes 1966080
Async XLA Ops:
  154.8 5.2 %copy-start = (bf16[4,10,12,1024]{3,2,1,0:T(8,128)(2,1)S(1)}, bf16[4,10,12,1024]{3,2,1,0:T(8,128)(2,1)}, u32[]{:S(2)}) copy-start(bf16[4,10,12,1024]{3,2,1,0:T(8,128)(2,1)} %get-tuple-element.99) | copy-start | bytes 2949124

commit v7 on v6

--- a/solution.py
+++ b/solution.py
@@ -196,12 +196,13 @@
         if s.direct:
 
             def send(step):
+                further = lax.rem(step + self.total // 4, self.total - 1)
                 pltpu.make_async_remote_copy(
                     s.pay,
                     s.near.at[self.me],
                     s.sems.at[0],
                     s.sems.at[1],
-                    device_id=self.device(lax.rem(self.me + step + 1, self.total)),
+                    device_id=self.device(lax.rem(self.me + further + 1, self.total)),
                     device_id_type=MESH,
                 ).start()
 

time: 162 us -> 162 us (level)
  no operation moved by 1% of the time
where the time goes in v7:
time: 162 us
  Pallas kernels  152 us (94%)
  local copies, waits for them, and re-layouts  8.95 us (6%)
    pallas_call x1, Pallas kernels, both_blocks(): pl.pallas_call(body, out_shape=parts[1], in_specs=spec_leaves[0], out_spe...  150 us
    unnamed x6, local copies, waits for them, and re-layouts  8.95 us

profile of v7, /device:TPU:0, one launch (start us, length us, event | category | flops | bytes accessed | tf_op | source)
XLA Modules:
  0.0 162.0 jit_solution(5633841364159357949)
XLA Ops:
  0.7 2.0 %copy.58 = bf16[2,12,5,2048]{3,1,2,0:T(8,128)(2,1)} copy(bf16[2,12,5,2048]{3,0,2,1:T(2,128)(2,1)} %param.51) | data formatting | bytes 983040 | tf_op args[25]
  2.7 2.8 %copy.57 = bf16[4,12,10,1024]{3,1,2,0:T(8,128)(2,1)} copy(bf16[4,12,10,1024]{3,0,2,1:T(4,128)(2,1)} %param.27) | data formatting | bytes 1966080 | tf_op args[1]
  5.5 149.6 %shard_map.441 = (f32[1,256]{1,0:T(1,128)}, f32[1,256]{1,0:T(1,128)}, f32[1,1024]{1,0:T(1,128)}, f32[1,512]{1,0:T(1,128)}, f32[1,512]{1,0:T(1,128)}, /*index=5*/...) custom-call(f32[1,256]{1,0:T(1,128)} %bitcast.85, ...), custom_call_target="tpu_custom_call" | custom-call | flops 16000000000 | bytes 30000000 | tf_op jit(solution)/shard_map/pallas_call | solution.py:1288
  155.2 0.0 copy-start
  155.2 2.8 %shard_map.442 = (bf16[2,7,4,2048]{3,2,1,0:T(4,128)(2,1)}, bf16[4,14,4,1024]{3,2,1,0:T(4,128)(2,1)}, f32[32,256]{1,0:T(8,128)}, f32[9,8,256]{2,1,0:T(8,128)}, f3...) custom-call(bf16[2,7,4,2048]{3,2,1,0:T(4,128)(2,1)} %get-tuple-eleme, ...), custom_call_target="tpu_custom_call" | custom-call | tf_op jit(solution)/shard_map/pallas_call | solution.py:1129
  157.9 2.4 %copy.53 = bf16[2,12,5,2048]{3,0,2,1:T(2,128)(2,1)} copy(bf16[2,12,5,2048]{3,1,2,0:T(8,128)(2,1)} %bitcast.55) | data formatting | bytes 983040
  160.3 0.0 copy-done
  160.3 1.7 %copy.54 = bf16[4,12,10,1024]{3,0,2,1:T(4,128)(2,1)} copy(bf16[4,12,10,1024]{3,1,2,0:T(8,128)(2,1)S(1)} %bitcast.53) | data formatting | bytes 1966080
Async XLA Ops:
  155.2 5.2 %copy-start = (bf16[4,10,12,1024]{3,2,1,0:T(8,128)(2,1)S(1)}, bf16[4,10,12,1024]{3,2,1,0:T(8,128)(2,1)}, u32[]{:S(2)}) copy-start(bf16[4,10,12,1024]{3,2,1,0:T(8,128)(2,1)} %get-tuple-element.99) | copy-start | bytes 2949124
